TPU v7x, 32 devices: a whole 2x2x4 slice. The times are simulated.
32 devices in a mesh: head: 8 (over z, y), tok: 4 (over x, core).
Axes of the slice: x: 2, y: 2, z: 4, core: 2. Of those that a mesh axis runs over, the one named last changes fastest.
Arguments:
- queries: bfloat16 [512, 8192], P('tok', 'head'), may hold values from -6 to 6
- cache: bfloat16 [4, 2048, 256], P(None, 'tok'), may hold values from -6 to 6
- new_kv: bfloat16 [4, 512, 256], P(None, 'tok'), may hold values from -6 to 6
- q_gain: float32 [128], replicated, may hold values from 0.5 to 2.2
- k_gain: float32 [128], replicated, may hold values from 0.5 to 2.2
- out_weight: bfloat16 [8192, 4096], P('head'), may hold values from -0.5 to 0.5
- residual: bfloat16 [512, 4096], P(('tok', 'head')), may hold values from -3 to 3
- norm_gain: float32 [4096], replicated, may hold values from 0.25 to 1.75
- expert_ids: int32 [512, 8], P(('tok', 'head')), may hold values from 0 to 31, all different within a row; in each aligned block of 16 rows (0 to 15, 16 to 31, ...) at most 8 rows name the same one
- combine_weight: bfloat16 [512, 8], P(('tok', 'head')), may hold values from 0.049804688 to 0.5
- prefix_len: int32 [1], replicated, may hold values from 1024 to 2048
- w_gate_up: bfloat16 [32, 4096, 1536], P(('head', 'tok')), may hold values from -0.09375 to 0.09375
- w_down: bfloat16 [32, 768, 4096], P(('head', 'tok')), may hold values from -0.21875 to 0.21875
Outputs:
- layer_out: bfloat16 [512, 4096], P(('tok', 'head'))
Inputs may be any that keep to these rules, and one draw needn't show every extreme that they name: `expert_ids`: in each aligned block of 16 rows (the rows of one device) no expert is named by more than 8 rows, and some expert reaches 8.
All inputs are finite; a program needn't handle non-finite values.
Results may differ from a plain program's by a relative error of at most 0.022.
Values may be sent and summed in bfloat16 or wider, within the bound.
A program may use at most 128 MiB of HBM per device.

v0:
```python
import jax
import jax.numpy as jnp
from jax import lax
from jax.sharding import PartitionSpec as P

HEADS = 64
KV_HEADS = 4
HD = 128


EPSILON = 1e-06


def rms_scale(values, gain):
    mean_square = jnp.mean(values * values, axis=-1, keepdims=True)
    return values * lax.rsqrt(mean_square + EPSILON) * gain


def expert_block(inputs, gate_up, down_proj):
    width = down_proj.shape[1]
    hidden_units = down_proj.shape[0]
    flat_rows = inputs.reshape(-1, width)
    both = jnp.dot(flat_rows, gate_up, preferred_element_type=jnp.float32)
    active = (jax.nn.silu(both[:, :hidden_units]) * both[:, hidden_units:]).astype(jnp.bfloat16)
    result = jnp.dot(active, down_proj, preferred_element_type=jnp.float32).astype(jnp.bfloat16)
    return result.reshape(inputs.shape)


def per_device(
    queries,
    cache,
    new_kv,
    q_gain,
    k_gain,
    out_weight,
    residual,
    norm_gain,
    expert_ids,
    combine_weight,
    prefix_len,
    w_gate_up,
    w_down,
):
    head_count = lax.axis_size("head")
    tok_count = lax.axis_size("tok")
    query_rows = queries.shape[0]
    local_heads = queries.shape[1] // HD
    cache_rows = cache.shape[1]
    segment = cache_rows + query_rows
    kv_index = lax.axis_index("head") * local_heads // (HEADS // KV_HEADS)
    query_normed = rms_scale(
        queries.reshape(query_rows, local_heads, HD).astype(jnp.float32), q_gain
    ).astype(jnp.bfloat16)
    own_block = jnp.concatenate(
        [
            lax.dynamic_index_in_dim(cache, kv_index, 0, keepdims=False),
            lax.dynamic_index_in_dim(new_kv, kv_index, 0, keepdims=False),
        ],
        axis=0,
    )
    key_part = rms_scale(own_block[:, :HD].astype(jnp.float32), k_gain).astype(jnp.bfloat16)
    key_block = jnp.concatenate([key_part, own_block[:, HD:]], axis=1)
    query_position = lax.axis_index("tok") * query_rows + jnp.arange(query_rows, dtype=jnp.int32)
    limit = prefix_len[0]
    piece = lax.all_gather(key_block, "tok", axis=0, tiled=True)
    position = jnp.arange(piece.shape[0], dtype=jnp.int32)
    shard = position // segment
    offset = position % segment
    in_cache = offset < cache_rows
    cache_position = shard * cache_rows + offset
    span_position = shard * query_rows + offset - cache_rows
    visible = jnp.where(
        in_cache[None, :],
        (cache_position < limit)[None, :],
        span_position[None, :] <= query_position[:, None],
    )
    scores = jnp.einsum(
        "qhd,kd->qhk", query_normed, piece[:, :HD], preferred_element_type=jnp.float32
    ) * HD ** (-0.5)
    weights = jnp.where(visible[:, None, :], jnp.exp(scores), 0.0)
    accum = jnp.einsum(
        "qhk,kd->qhd",
        weights.astype(jnp.bfloat16),
        piece[:, HD:],
        preferred_element_type=jnp.float32,
    )
    total = jnp.sum(weights, axis=2)
    accum, total = (accum, total)
    attn = (accum / total[:, :, None]).astype(jnp.bfloat16).reshape(query_rows, local_heads * HD)
    rows_out = query_rows // head_count
    full_proj = lax.psum(
        jnp.dot(attn, out_weight, preferred_element_type=jnp.float32).astype(jnp.bfloat16), "head"
    ).astype(jnp.float32)
    attn_proj = lax.dynamic_slice_in_dim(full_proj, lax.axis_index("head") * rows_out, rows_out, 0)
    hidden = residual.astype(jnp.float32) + attn_proj
    normed = rms_scale(hidden, norm_gain).astype(jnp.bfloat16)
    width = normed.shape[1]
    experts_all = head_count * tok_count
    topk = expert_ids.shape[1]
    capacity = max(2, 2 * rows_out * topk // experts_all)
    flat_ids = expert_ids.reshape(-1)
    onehot = (flat_ids[:, None] == jnp.arange(experts_all, dtype=jnp.int32)[None, :]).astype(
        jnp.int32
    )
    before = jnp.cumsum(onehot, axis=0) - onehot
    slot_index = jnp.sum(before * onehot, axis=1)
    target = (flat_ids * capacity + slot_index).reshape(rows_out, topk)
    matches = (
        target[:, :, None] == jnp.arange(experts_all * capacity, dtype=jnp.int32)[None, None, :]
    )
    placing = jnp.sum(matches.astype(jnp.int32), axis=1).astype(jnp.bfloat16)
    mixing = jnp.sum(
        jnp.where(matches, combine_weight.astype(jnp.float32)[:, :, None], 0.0), axis=1
    ).astype(jnp.bfloat16)
    outgoing = jnp.einsum("rs,rd->sd", placing, normed, preferred_element_type=jnp.float32).astype(
        jnp.bfloat16
    )
    outgoing = outgoing.reshape(experts_all, capacity, width)
    returned = lax.all_to_all(
        expert_block(
            lax.all_to_all(outgoing, ("head", "tok"), split_axis=0, concat_axis=0, tiled=True),
            w_gate_up[0],
            w_down[0],
        ),
        ("head", "tok"),
        split_axis=0,
        concat_axis=0,
        tiled=True,
    )
    back_rows = returned.reshape(experts_all * capacity, width)
    expert_sum = jnp.dot(mixing, back_rows, preferred_element_type=jnp.float32)
    return (hidden + expert_sum).astype(jnp.bfloat16)


def solution(mesh):
    placed = (
        P("tok", "head"),
        P(None, "tok", None),
        P(None, "tok", None),
        P(),
        P(),
        P("head", None),
        P(("tok", "head"), None),
        P(),
        P(("tok", "head"), None),
        P(("tok", "head"), None),
        P(),
        P(("head", "tok"), None, None),
        P(("head", "tok"), None, None),
    )
    return jax.shard_map(
        per_device, mesh=mesh, in_specs=placed, out_specs=P(("tok", "head"), None), check_vma=False
    )
```

profile of v0, /device:TPU:0, one launch (start us, length us, event | category | flops | bytes accessed | tf_op | source)
XLA Modules:
  0.0 245.2 jit_solution(4401951425939910225)
XLA Ops:
  6.5 0.0 copy-start
  6.5 0.0 copy-start.5
  6.5 0.0 all-gather.2.cloned.1.call-start
  6.5 1.2 copy-done
  7.8 0.9 dynamic-slice_bitcast_fusion.1
  8.6 0.2 fusion.31
  8.8 0.8 fusion.33
  9.6 0.8 fusion.35
  10.4 0.0 all-gather.2.cloned.1.call-update
  10.4 0.0 all-reduce.2.cloned.1.call-start
  11.1 1.0 convert_bitcast_fusion
  12.1 0.1 copy.43
  12.2 0.2 multiply_reduce_fusion
  12.5 0.1 copy.35
  12.7 0.0 copy-done.5
  12.7 0.2 multiply_convert_fusion
  12.9 0.3 compare_select_fusion
  13.2 18.3 %all-gather.2.cloned.1.call-done = bf16[2560,256]{1,0:T(8,128)(2,1)} async-done(((bf16[640,256]{1,0:T(8,128)(2,1)}), bf16[2560,256]{1,0:T(8,128)(2,1)}) %all-gather.2.cloned.1.call-update) | async-done | bytes 1310736 | tf_op jit(solution)/shard_map/all_gather | solution.py:65
  31.5 0.0 copy-start.6
  31.5 0.0 slice-start
  31.5 4.1 %fusion.2 = (f32[128,8]{0,1:T(8,128)S(1)}, f32[128,8,2560]{2,0,1:T(8,128)S(1)}) fusion(pred[128,2560]{1,0:T(8,128)(4,1)S(1)} %compare_select_fusion, bf16[2560,256]{1,0:T(8,128)(2,1)} %all-gather.2.cloned.1.call-done, bf16[128,8,128]{2,1,0:T(8,128)(2,1)S(1)} %multiply_convert_fusion), kind=kOutput, calls=%fused_computation.3 | convolution fusion | flops 678951936 | bytes 11735040 | tf_op jit(solution)/shard_map/qhd,kd->qhk/dot_general | solution.py:77
  35.6 0.0 copy-done.6
  35.6 0.0 slice-start.1
  35.6 2.0 fusion.22
  37.6 0.0 slice-done
  37.6 0.2 slice-done.1
  37.8 0.0 copy-start.3
  37.8 0.0 copy-start.1
  37.8 0.0 copy-start.2
  37.8 2.3 convolution_convert_fusion.1
  40.1 0.0 all-reduce.2.cloned.1.call-update
  40.1 0.0 copy-done.3
  40.1 0.1 copy.38
  40.2 0.1 eq.30
  40.3 0.1 fusion.41
  40.4 0.2 reduce_window_sum.11
  40.6 0.2 select_reduce_fusion.1
  40.7 0.1 reduce_sum.69
  40.8 0.1 convert_reduce_fusion
  41.0 77.5 %all-reduce.2.cloned.1.call-done = bf16[128,4096]{1,0:T(8,128)(2,1)} async-done(((bf16[128,4096]{1,0:T(8,128)(2,1)}), bf16[128,4096]{1,0:T(8,128)(2,1)}) %all-reduce.2.cloned.1.call-update) | async-done | bytes 1048592 | tf_op jit(solution)/shard_map/psum | solution.py:91
  118.5 0.0 copy-done.1
  118.5 1.1 multiply_reduce_fusion.1
  119.5 0.0 copy-done.2
  119.6 1.7 fusion.15
  121.2 0.0 slice-start.2
  121.2 52.7 %all_to_all.10 = bf16[32,8,4096]{2,1,0:T(8,128)(2,1)S(1)} all-to-all(bf16[32,8,4096]{2,1,0:T(8,128)(2,1)S(1)} %fusion.15), channel_id=1, replica_groups=mesh['head'=8,'tok'=4] {'head','tok'}, dimensions={0} | all-to-all | bytes 4194304 | tf_op jit(solution)/shard_map/all_to_all | solution.py:121
  173.9 0.0 slice-start.3
  173.9 6.6 %fusion = f32[256,1536]{1,0:T(8,128)S(1)} fusion(bf16[1,4096,1536]{2,1,0:T(8,128)(2,1)} %param.24, bf16[32,8,4096]{2,1,0:T(8,128)(2,1)S(1)} %all_to_all.10), kind=kOutput, calls=%fused_computation | convolution fusion | flops 3221225472 | bytes 16252928 | tf_op jit(solution)/shard_map/dot_general | solution.py:23
  180.5 0.0 slice-done.2
  180.5 0.0 slice-done.3
  180.6 0.0 copy-start.4
  180.6 3.2 %fusion.12 = bf16[32,8,4096]{2,1,0:T(8,128)(2,1)} fusion(bf16[1,768,4096]{2,1,0:T(8,128)(2,1)S(1)} %bitcast.47, f32[256,1536]{1,0:T(8,128)S(1)} %fusion), kind=kOutput, calls=%fused_computation.11 | convolution fusion | flops 1612840960 | bytes 9961472 | tf_op jit(solution)/shard_map/dot_general | solution.py:25
  183.8 3.7 %all-to-all-start.1 = ((bf16[32,8,4096]{2,1,0:T(8,128)(2,1)}), bf16[32,8,4096]{2,1,0:T(8,128)(2,1)S(1)}, u32[]{:S(2)}, u32[]{:S(2)}) async-start(bf16[32,8,4096]{2,1,0:T(8,128)(2,1)} %fusion.12), calls=%async_computation.1 | async-start | bytes 4194304 | tf_op jit(solution)/shard_map/all_to_all | solution.py:119
  187.5 0.0 copy-done.4
  187.5 0.1 copy.40
  187.6 0.1 select_reduce_fusion
  187.7 48.7 %all-to-all-done.1 = bf16[32,8,4096]{2,1,0:T(8,128)(2,1)S(1)} async-done(((bf16[32,8,4096]{2,1,0:T(8,128)(2,1)}), bf16[32,8,4096]{2,1,0:T(8,128)(2,1)S(1)}, u32[]{:S(2)}, u32[]{:S(2)}) %all-to-all-start.1) | async-done | bytes 2097184 | tf_op jit(solution)/shard_map/all_to_all | solution.py:119
  236.4 2.0 fusion.16
  (11 shorter events, 0.1 us)
Async XLA Ops:
  6.5 1.2 copy-start
  6.5 6.2 %copy-start.5 = (f32[128]{0:T(128)S(1)}, f32[128]{0:T(128)}, u32[]{:S(2)}) copy-start(f32[128]{0:T(128)} %param.16) | copy-start | bytes 1540
  6.5 24.9 %all-gather.2.cloned.1.call-start = ((), (), s32[]{:S(2)}) async-start(), calls=%async_computation.2 | async-start | bytes 1638400 | tf_op jit(solution)/shard_map/all_gather | solution.py:65
  10.4 108.0 %all-reduce.2.cloned.1.call-start = ((), (), s32[]{:S(2)}) async-start(), calls=%async_computation.3 | async-start | bytes 2097152 | tf_op jit(solution)/shard_map/psum | solution.py:91
  31.5 4.1 %copy-start.6 = (bf16[2560,256]{1,0:T(8,128)(2,1)S(1)}, bf16[2560,256]{1,0:T(8,128)(2,1)}, u32[]{:S(2)}) copy-start(bf16[2560,256]{1,0:T(8,128)(2,1)} %all-gather.2.cloned.1.call-done) | copy-start | bytes 3932164
  31.5 6.1 %slice-start = ((s8[8388608]{0:T(1024)(128)(4,1)}), s8[4194304]{0:T(1024)(128)(4,1)S(1)}, s32[]{:S(2)}) async-start(s8[8388608]{0:T(1024)(128)(4,1)} %bitcast.42), calls=%async_computation.4 | async-start | bytes 8388608
  35.6 2.2 slice-start.1
  37.8 2.3 copy-start.3
  37.8 80.7 %copy-start.1 = (bf16[16,4096]{1,0:T(8,128)(2,1)S(1)}, bf16[16,4096]{1,0:T(8,128)(2,1)}, u32[]{:S(2)}) copy-start(bf16[16,4096]{1,0:T(8,128)(2,1)} %param.19) | copy-start | bytes 393220
  37.8 81.7 %copy-start.2 = (f32[4096]{0:T(1024)S(1)}, f32[4096]{0:T(1024)}, u32[]{:S(2)}) copy-start(f32[4096]{0:T(1024)} %param.20) | copy-start | bytes 49156
  121.2 59.3 %slice-start.2 = ((s8[6291456]{0:T(1024)(128)(4,1)}), s8[4194304]{0:T(1024)(128)(4,1)S(1)}, s32[]{:S(2)}) async-start(s8[6291456]{0:T(1024)(128)(4,1)} %bitcast.46), calls=%async_computation.6 | async-start | bytes 8388608
  173.9 6.6 %slice-start.3 = ((s8[6291456]{0:T(1024)(128)(4,1)}), s8[2097152]{0:T(1024)(128)(4,1)S(1)}, s32[]{:S(2)}) async-start(s8[6291456]{0:T(1024)(128)(4,1)} %bitcast.46), calls=%async_computation.7 | async-start | bytes 4194304
  180.6 6.9 %copy-start.4 = (bf16[16,8]{0,1:T(8,128)(2,1)S(1)}, bf16[16,8]{0,1:T(8,128)(2,1)}, u32[]{:S(2)}) copy-start(bf16[16,8]{0,1:T(8,128)(2,1)} %param.22) | copy-start | bytes 772
  183.8 52.6 %all-to-all-start.1 = ((bf16[32,8,4096]{2,1,0:T(8,128)(2,1)}), bf16[32,8,4096]{2,1,0:T(8,128)(2,1)S(1)}, u32[]{:S(2)}, u32[]{:S(2)}) async-start(bf16[32,8,4096]{2,1,0:T(8,128)(2,1)} %fusion.12), calls=%async_computation.1 | async-start | bytes 4194304 | tf_op jit(solution)/shard_map/all_to_all | solution.py:119
Sparse Core Ops, SparseCore 0:
  10.6 20.8 all-gather.1
  40.2 78.1 all-reduce.1
where the time goes:
time: 246 us; the launch traced here: 245 us
  waiting for transfers between devices  144 us (59%)
  blocking collectives  52.7 us (21%)
  matrix products  21.8 us (9%)
  between operations  14.3 us (6%)
  other arithmetic  5.27 us (2%)
  starting transfers between devices  3.7 us (2%)
  local copies, waits for them, and re-layouts  2.9 us (1%)
    psum x1, waiting for transfers between devices, per_device(): lax.psum(jnp.dot(attn, out_weight, preferred_element_type=jnp.float32).as...  77.5 us
    all_to_all x1, blocking collectives, per_device(): lax.all_to_all(outgoing, ('head', 'tok'), split_axis=0, concat_axis=0, ti...  52.7 us
    all_to_all x1, waiting for transfers between devices, per_device(): lax.all_to_all(expert_block(lax.all_to_all(outgoing, ('head', 'tok'), spl...  48.7 us
    all_gather x1, waiting for transfers between devices, per_device(): piece = lax.all_gather(key_block, 'tok', axis=0, tiled=True)  18.3 us
    dot_general x1, matrix products, expert_block(): both = jnp.dot(flat_rows, gate_up, preferred_element_type=jnp.float32)  6.58 us
  transfers between devices with their start and end apart: 3, of which 3 were waited for; matrix products, arithmetic and copies ran while one was open for 1% of the time, Pallas kernels for 0%

commit v1 on v0

--- a/solution.py
+++ b/solution.py
@@ -1,6 +1,10 @@
+import functools
+
 import jax
 import jax.numpy as jnp
 from jax import lax
+from jax.experimental import pallas as pl
+from jax.experimental.pallas import tpu as pltpu
 from jax.sharding import PartitionSpec as P
 
 HEADS = 64
@@ -24,6 +28,352 @@
     active = (jax.nn.silu(both[:, :hidden_units]) * both[:, hidden_units:]).astype(jnp.bfloat16)
     result = jnp.dot(active, down_proj, preferred_element_type=jnp.float32).astype(jnp.bfloat16)
     return result.reshape(inputs.shape)
+
+
+DEPTH = 4
+CORES = 2
+CHUNKS = 4
+VMEM_BYTES = 60 * 2**20
+MESH = pl.DeviceIdType.MESH
+
+
+def dot32(a, b):
+    return jnp.dot(a, b, preferred_element_type=jnp.float32)
+
+
+def layer_kernel(
+    dims,
+    attn_ref,
+    out_weight_hbm,
+    residual_ref,
+    gain_ref,
+    place_row_ref,
+    place_col_ref,
+    scale_col_ref,
+    gate_up_hbm,
+    down_hbm,
+    result_ref,
+    out_w,
+    gate_up,
+    down,
+    part,
+    part_y,
+    sum_y,
+    part_z,
+    hidden,
+    rows,
+    acc,
+    active,
+    share,
+    in_core,
+    sum_core,
+    in_ax,
+    in_ay,
+    sum_ax,
+    sum_ay,
+    in_bx,
+    in_by,
+    sum_b,
+    in_z,
+    load_sem,
+    send_sem,
+    recv_sem,
+):
+    nz, ny, nx, slots = dims
+    head, tok = lax.axis_index("head"), lax.axis_index("tok")
+    z, y = lax.div(head, ny), lax.rem(head, ny)
+    x, core = lax.div(tok, CORES), lax.rem(tok, CORES)
+    width = hidden.shape[1]
+    step = width // CHUNKS
+    tokens = place_row_ref.shape[1]
+    hidden_units = down.shape[0]
+    columns = [pl.ds(k * step, step) for k in range(CHUNKS)]
+
+    axes = {
+        "z": (nz, z, lambda p: (p * ny + y, tok)),
+        "y": (ny, y, lambda p: (z * ny + p, tok)),
+        "x": (nx, x, lambda p: (head, p * CORES + core)),
+        "core": (CORES, core, lambda p: (head, x * CORES + p)),
+    }
+
+    loads = []
+
+    def load(src, dst):
+        copy = pltpu.make_async_copy(src, dst, load_sem.at[len(loads)])
+        copy.start()
+        loads.append(copy)
+        return copy
+
+    out_w_loads = [load(out_weight_hbm.at[:, c], out_w.at[:, c]) for c in columns]
+    gate_up_loads = [load(gate_up_hbm.at[0, c, :], gate_up.at[c, :]) for c in columns]
+    down_loads = [load(down_hbm.at[0, :, c], down.at[:, c]) for c in columns]
+
+    barrier = pltpu.get_barrier_semaphore()
+    greeted = 0
+    for n, me, device in axes.values():
+        for i in range(1, n):
+            pl.semaphore_signal(
+                barrier, inc=1, device_id=device(lax.rem(me + i, n)), device_id_type=MESH
+            )
+            greeted += 1
+    pl.semaphore_wait(barrier, greeted)
+
+    sends = []
+
+    def send(stage, k, axis, source, target):
+        n, me, device = axes[axis]
+        for i in range(1, n):
+            peer = lax.rem(me + i, n)
+            copy = pltpu.make_async_remote_copy(
+                src_ref=source(peer),
+                dst_ref=target(i),
+                send_sem=send_sem.at[stage, k, i - 1],
+                recv_sem=recv_sem.at[stage, k, i - 1],
+                device_id=device(peer),
+                device_id_type=MESH,
+            )
+            copy.start()
+            sends.append(copy)
+
+    def arrive(stage, k, axis, region):
+        n, me, device = axes[axis]
+        for i in range(1, n):
+            peer = lax.rem(me + n - i, n)
+            place = region(i, peer)
+            pltpu.make_async_remote_copy(
+                src_ref=place,
+                dst_ref=place,
+                send_sem=send_sem.at[stage, k, i - 1],
+                recv_sem=recv_sem.at[stage, k, i - 1],
+                device_id=device(peer),
+                device_id_type=MESH,
+            ).wait_recv()
+
+    def total(first, others):
+        value = first.astype(jnp.float32)
+        for other in others:
+            value = value + other.astype(jnp.float32)
+        return value
+
+    for k, c in enumerate(columns):
+        out_w_loads[k].wait()
+        proj = dot32(attn_ref[...], out_w[:, c]).astype(jnp.bfloat16)
+        part[:, :, :, c] = proj.reshape(nz, ny, -1, step)
+        send(0, k, "y", lambda p: part.at[:, p, :, c], lambda i: part_y.at[i - 1, :, :, c])
+    for k, c in enumerate(columns):
+        arrive(0, k, "y", lambda i, p: part_y.at[i - 1, :, :, c])
+        value = total(part[:, y, :, c], [part_y[i, :, :, c] for i in range(ny - 1)])
+        sum_y[:, :, c] = value.astype(jnp.bfloat16)
+        send(1, k, "z", lambda p: sum_y.at[p, :, c], lambda i: part_z.at[i - 1, :, c])
+    square = jnp.zeros((hidden.shape[0], 1), jnp.float32)
+    for k, c in enumerate(columns):
+        arrive(1, k, "z", lambda i, p: part_z.at[i - 1, :, c])
+        value = total(sum_y[z, :, c], [part_z[i, :, c] for i in range(nz - 1)])
+        value = value + residual_ref[:, c].astype(jnp.float32)
+        hidden[:, c] = value
+        square = square + jnp.sum(value * value, axis=1, keepdims=True)
+    scale = lax.rsqrt(square / width + EPSILON)
+
+    for k, c in enumerate(columns):
+        rows[tok, z, y, :, c] = (hidden[:, c] * scale * gain_ref[:, c]).astype(jnp.bfloat16)
+        mine = lambda _: rows.at[tok, z, y, :, c]
+        send(2, k, "z", mine, mine)
+    for k, c in enumerate(columns):
+        arrive(2, k, "z", lambda i, p: rows.at[tok, p, y, :, c])
+        mine = lambda _: rows.at[tok, :, y, :, c]
+        send(3, k, "xy"[k % 2], mine, mine)
+    for k, c in enumerate(columns):
+        if k % 2 == 0:
+            arrive(3, k, "x", lambda i, p: rows.at[p * CORES + core, :, y, :, c])
+            for q in range(nx):
+                mine = lambda _: rows.at[q * CORES + core, :, y, :, c]
+                send(4 + q, k, "y", mine, mine)
+        else:
+            arrive(3, k, "y", lambda i, p: rows.at[tok, :, p, :, c])
+            mine = lambda _: rows.at[tok, :, :, :, c]
+            send(4, k, "x", mine, mine)
+    base = 4 + nx
+    for k, c in enumerate(columns):
+        if k % 2 == 0:
+            for q in range(nx):
+                arrive(4 + q, k, "y", lambda i, p: rows.at[q * CORES + core, :, p, :, c])
+        else:
+            arrive(4, k, "x", lambda i, p: rows.at[p * CORES + core, :, :, :, c])
+        for q in range(nx):
+            mine = lambda _: rows.at[q * CORES + core, :, :, :, c]
+            send(base + q, k, "core", mine, mine)
+    select = (
+        lax.broadcasted_iota(jnp.int32, (slots, tokens), 0) == place_row_ref[...]
+    ).astype(jnp.bfloat16)
+    for k, c in enumerate(columns):
+        for q in range(nx):
+            arrive(base + q, k, "core", lambda i, p: rows.at[q * CORES + p, :, :, :, c])
+        picked = dot32(select, rows[:, :, :, :, c].reshape(tokens, step)).astype(jnp.bfloat16)
+        gate_up_loads[k].wait()
+        both = dot32(picked, gate_up[c, :])
+        acc[...] = both if k == 0 else acc[...] + both
+    base += nx
+
+    gate = acc[:, :hidden_units]
+    active[...] = (jax.nn.silu(gate) * acc[:, hidden_units:]).astype(jnp.bfloat16)
+    spread = jnp.where(
+        lax.broadcasted_iota(jnp.int32, (tokens, slots), 1) == place_col_ref[...],
+        scale_col_ref[...],
+        0.0,
+    ).astype(jnp.bfloat16)
+
+    for k, c in enumerate(columns):
+        down_loads[k].wait()
+        expert_out = dot32(active[...], down[:, c]).astype(jnp.bfloat16)
+        weighted = dot32(spread, expert_out).astype(jnp.bfloat16)
+        share[:, :, :, :, :, c] = weighted.reshape(nx, CORES, nz, ny, -1, step)
+        send(
+            base, k, "core",
+            lambda p: share.at[:, p, :, :, :, c],
+            lambda i: in_core.at[:, :, :, :, c],
+        )
+    for k, c in enumerate(columns):
+        arrive(base, k, "core", lambda i, p: in_core.at[:, :, :, :, c])
+        value = total(share[:, core, :, :, :, c], [in_core[:, :, :, :, c]])
+        sum_core[:, :, :, :, c] = value.astype(jnp.bfloat16)
+        if k % 2 == 0:
+            send(
+                base + 1, k, "x",
+                lambda p: sum_core.at[p, :, :, :, c],
+                lambda i: in_ax.at[i - 1, :, :, :, c],
+            )
+        else:
+            send(
+                base + 1, k, "y",
+                lambda p: sum_core.at[:, :, p, :, c],
+                lambda i: in_ay.at[i - 1, :, :, :, c],
+            )
+    for k, c in enumerate(columns):
+        if k % 2 == 0:
+            arrive(base + 1, k, "x", lambda i, p: in_ax.at[i - 1, :, :, :, c])
+            value = total(
+                sum_core[x, :, :, :, c], [in_ax[i, :, :, :, c] for i in range(nx - 1)]
+            )
+            sum_ax[:, :, :, c] = value.astype(jnp.bfloat16)
+            send(
+                base + 2, k, "y",
+                lambda p: sum_ax.at[:, p, :, c],
+                lambda i: in_by.at[i - 1, :, :, c],
+            )
+        else:
+            arrive(base + 1, k, "y", lambda i, p: in_ay.at[i - 1, :, :, :, c])
+            value = total(
+                sum_core[:, :, y, :, c], [in_ay[i, :, :, :, c] for i in range(ny - 1)]
+            )
+            sum_ay[:, :, :, c] = value.astype(jnp.bfloat16)
+            send(
+                base + 2, k, "x",
+                lambda p: sum_ay.at[p, :, :, c],
+                lambda i: in_bx.at[i - 1, :, :, c],
+            )
+    for k, c in enumerate(columns):
+        if k % 2 == 0:
+            arrive(base + 2, k, "y", lambda i, p: in_by.at[i - 1, :, :, c])
+            value = total(sum_ax[:, y, :, c], [in_by[i, :, :, c] for i in range(ny - 1)])
+        else:
+            arrive(base + 2, k, "x", lambda i, p: in_bx.at[i - 1, :, :, c])
+            value = total(sum_ay[x, :, :, c], [in_bx[i, :, :, c] for i in range(nx - 1)])
+        sum_b[:, :, c] = value.astype(jnp.bfloat16)
+        send(base + 3, k, "z", lambda p: sum_b.at[p, :, c], lambda i: in_z.at[i - 1, :, c])
+    for k, c in enumerate(columns):
+        arrive(base + 3, k, "z", lambda i, p: in_z.at[i - 1, :, c])
+        value = total(sum_b[z, :, c], [in_z[i, :, c] for i in range(nz - 1)])
+        result_ref[:, c] = (hidden[:, c] + value).astype(jnp.bfloat16)
+    for copy in sends:
+        copy.wait_send()
+
+
+def routed_layer(
+    attn, out_weight, residual, norm_gain, expert_ids, combine_weight, w_gate_up, w_down
+):
+    head_count = lax.axis_size("head")
+    tok_count = lax.axis_size("tok")
+    nz, ny, nx = DEPTH, head_count // DEPTH, tok_count // CORES
+    width = out_weight.shape[1]
+    rows_out, topk = expert_ids.shape
+    experts_all = head_count * tok_count
+    tokens = rows_out * experts_all
+    capacity = max(2, 2 * rows_out * topk // experts_all)
+    slots = experts_all * capacity
+    hidden_units = w_down.shape[1]
+
+    routing = lax.all_gather(
+        jnp.concatenate([expert_ids.astype(jnp.bfloat16), combine_weight], axis=1),
+        ("tok", "head"),
+        axis=0,
+        tiled=True,
+    )
+    own = lax.axis_index("head") * tok_count + lax.axis_index("tok")
+    named = routing[:, :topk].astype(jnp.int32) == own
+    chosen = jnp.any(named, axis=1)
+    scale = jnp.sum(jnp.where(named, routing[:, topk:].astype(jnp.float32), 0.0), axis=1)
+    blocks = chosen.reshape(experts_all, rows_out).astype(jnp.int32)
+    earlier = jnp.arange(rows_out)[:, None] < jnp.arange(rows_out)[None, :]
+    before = jnp.sum(jnp.where(earlier[None], blocks[:, :, None], 0), axis=1)
+    place = jnp.arange(experts_all, dtype=jnp.int32)[:, None] * capacity + before
+    place = jnp.where(chosen, place.reshape(-1), -1)
+
+    b16, f32 = jnp.bfloat16, jnp.float32
+    vmem = pl.BlockSpec(memory_space=pltpu.VMEM)
+    hbm = pl.BlockSpec(memory_space=pl.ANY)
+    stages = 8 + 2 * nx
+    widest = max(nz, ny, nx, CORES) - 1
+    scratch = [
+        pltpu.VMEM(out_weight.shape, b16),
+        pltpu.VMEM(w_gate_up.shape[1:], b16),
+        pltpu.VMEM(w_down.shape[1:], b16),
+        pltpu.VMEM((nz, ny, rows_out, width), b16),
+        pltpu.VMEM((ny - 1, nz, rows_out, width), b16),
+        pltpu.VMEM((nz, rows_out, width), b16),
+        pltpu.VMEM((nz - 1, rows_out, width), b16),
+        pltpu.VMEM((rows_out, width), f32),
+        pltpu.VMEM((tok_count, nz, ny, rows_out, width), b16),
+        pltpu.VMEM((slots, 2 * hidden_units), f32),
+        pltpu.VMEM((slots, hidden_units), b16),
+        pltpu.VMEM((nx, CORES, nz, ny, rows_out, width), b16),
+        pltpu.VMEM((nx, nz, ny, rows_out, width), b16),
+        pltpu.VMEM((nx, nz, ny, rows_out, width), b16),
+        pltpu.VMEM((nx - 1, nz, ny, rows_out, width), b16),
+        pltpu.VMEM((ny - 1, nx, nz, rows_out, width), b16),
+        pltpu.VMEM((nz, ny, rows_out, width), b16),
+        pltpu.VMEM((nx, nz, rows_out, width), b16),
+        pltpu.VMEM((nx - 1, nz, rows_out, width), b16),
+        pltpu.VMEM((ny - 1, nz, rows_out, width), b16),
+        pltpu.VMEM((nz, rows_out, width), b16),
+        pltpu.VMEM((nz - 1, rows_out, width), b16),
+        pltpu.SemaphoreType.DMA((3 * CHUNKS,)),
+        pltpu.SemaphoreType.DMA((stages, CHUNKS, widest)),
+        pltpu.SemaphoreType.DMA((stages, CHUNKS, widest)),
+    ]
+    return pl.pallas_call(
+        functools.partial(layer_kernel, (nz, ny, nx, slots)),
+        out_shape=jax.ShapeDtypeStruct((rows_out, width), b16),
+        in_specs=[vmem, hbm, vmem, vmem, vmem, vmem, vmem, hbm, hbm],
+        out_specs=vmem,
+        scratch_shapes=scratch,
+        compiler_params=pltpu.CompilerParams(
+            collective_id=0, has_side_effects=True, vmem_limit_bytes=VMEM_BYTES
+        ),
+    )(
+        attn,
+        out_weight,
+        residual,
+        norm_gain.reshape(1, width),
+        place.reshape(1, tokens),
+        place.reshape(tokens, 1),
+        scale.reshape(tokens, 1),
+        w_gate_up,
+        w_down,
+    )
+
+
+def fits(tokens, width, experts):
+    return 12 * tokens * width <= VMEM_BYTES // 2 and experts <= 256
 
 
 def per_device(
@@ -87,6 +437,11 @@
     total = jnp.sum(weights, axis=2)
     accum, total = (accum, total)
     attn = (accum / total[:, :, None]).astype(jnp.bfloat16).reshape(query_rows, local_heads * HD)
+    experts_total = head_count * tok_count
+    if fits(query_rows * tok_count, out_weight.shape[1], experts_total):
+        return routed_layer(
+            attn, out_weight, residual, norm_gain, expert_ids, combine_weight, w_gate_up, w_down
+        )
     rows_out = query_rows // head_count
     full_proj = lax.psum(
         jnp.dot(attn, out_weight, preferred_element_type=jnp.float32).astype(jnp.bfloat16), "head"
@@ -130,7 +485,6 @@
     back_rows = returned.reshape(experts_all * capacity, width)
     expert_sum = jnp.dot(mixing, back_rows, preferred_element_type=jnp.float32)
     return (hidden + expert_sum).astype(jnp.bfloat16)
-
 
 def solution(mesh):
     placed = (

time: 246 us -> 192 us (0.78)
  waiting for transfers between devices: 144 us -> 0.04 us
  Pallas kernels: 0 us -> 86.5 us
  blocking collectives: 52.7 us -> 70.6 us
  matrix products: 21.8 us -> 6.22 us
  starting transfers between devices: 3.7 us -> 0.01 us
  local copies, waits for them, and re-layouts: 2.9 us -> 6.19 us
    pallas_call x0 -> x1, Pallas kernels: none -> 86.5 us  [routed_layer(): pl.pallas_call(functools.partial(layer_kernel, (nz, ny, nx, slots)), out_...]
    psum x1 -> x0, waiting for transfers between devices: 77.5 us -> none  [per_device(): lax.psum(jnp.dot(attn, out_weight, preferred_element_type=jnp.float32).as...]
    all_gather x0 -> x1, blocking collectives: none -> 70.6 us  [routed_layer(): lax.all_gather(jnp.concatenate([expert_ids.astype(jnp.bfloat16), combine_...]
    all_to_all x1 -> x0, blocking collectives: 52.7 us -> none  [per_device(): lax.all_to_all(outgoing, ('head', 'tok'), split_axis=0, concat_axis=0, ti...]
    all_to_all x1 -> x0, waiting for transfers between devices: 48.7 us -> none  [per_device(): lax.all_to_all(expert_block(lax.all_to_all(outgoing, ('head', 'tok'), spl...]
    all_gather x1, waiting for transfers between devices: 18.3 us -> 0.02 us  [per_device(): piece = lax.all_gather(key_block, 'tok', axis=0, tiled=True)]
    dot_general x5 -> x0, matrix products: 15.7 us -> none  [the longest x1 6.58 us: expert_block(): both = jnp.dot(flat_rows, gate_up, preferred_element_type=jnp.float32)]
    all_to_all x1 -> x0, starting transfers between devices: 3.66 us -> none  [per_device(): lax.all_to_all(expert_block(lax.all_to_all(outgoing, ('head', 'tok'), spl...]
  transfers between devices with their start and end apart: 3 -> 1, of which waited for: 3 -> 0; matrix products, arithmetic and copies ran while one was open for 1% -> 4% of each run, Pallas kernels for 0% -> 0%
where the time goes in v1:
time: 192 us; the launch traced here: 191 us
  Pallas kernels  86.5 us (45%)
  blocking collectives  70.6 us (37%)
  between operations  14.2 us (7%)
  other arithmetic  7.45 us (4%)
  matrix products  6.22 us (3%)
  local copies, waits for them, and re-layouts  6.19 us (3%)
    pallas_call x1, Pallas kernels, routed_layer(): pl.pallas_call(functools.partial(layer_kernel, (nz, ny, nx, slots)), out_...  86.5 us
    all_gather x1, blocking collectives, routed_layer(): lax.all_gather(jnp.concatenate([expert_ids.astype(jnp.bfloat16), combine_...  70.6 us
    dot_general x1, matrix products, per_device(): jnp.einsum('qhd,kd->qhk', query_normed, piece[:, :HD], preferred_element_...  4.25 us
  transfers between devices with their start and end apart: 1, of which 0 were waited for; matrix products, arithmetic and copies ran while one was open for 4% of the time, Pallas kernels for 0%

profile of v1, /device:TPU:0, one launch (start us, length us, event | category | flops | bytes accessed | tf_op | source)
XLA Modules:
  0.0 191.2 jit_solution(11722958716001570258)
XLA Ops:
  6.5 0.0 copy-start
  6.5 0.0 all-gather.2.cloned.1.call-start
  6.5 1.2 copy-done
  7.8 0.9 dynamic-slice_bitcast_fusion.1
  8.6 0.2 fusion.14
  8.8 0.8 fusion.16
  9.6 0.8 fusion.18
  10.4 0.0 all-gather.2.cloned.1.call-update
  10.5 0.7 convert_element_type.47
  11.2 0.7 pad_maximum_fusion
  11.8 0.1 copy.47
  11.9 70.6 %all_gather.7 = bf16[512,16]{1,0:T(8,128)(2,1)S(1)} all-gather(bf16[16,16]{1,0:T(8,128)(2,1)S(1)} %copy.47), channel_id=1, replica_groups=mesh['head'=8,'tok'=4] {'tok','head'}, dimensions={0}, use_global_device_ids=true | all-gather | bytes 16896 | tf_op jit(solution)/shard_map/all_gather | solution.py:305
  82.5 0.2 fusion.27
  82.7 0.1 reshape.195
  82.8 0.1 copy.48
  82.8 0.1 select_reduce_fusion.1
  83.0 0.1 copy.49
  83.0 0.2 add.133
  83.2 0.1 add.131
  84.0 1.0 convert_bitcast_fusion
  85.0 0.1 copy.57
  85.1 0.2 multiply_reduce_fusion
  85.3 0.1 copy.43
  85.5 0.2 select_reduce_fusion
  85.7 0.9 copy.53.scale_col_ref
  86.6 0.6 reshape_select_fusion.1.place_row_ref
  87.2 0.8 reshape_select_fusion.place_col_ref
  88.0 0.9 multiply_convert_fusion
  88.9 0.3 compare_select_fusion
  89.2 0.0 all-gather.2.cloned.1.call-done
  89.2 0.0 copy-start.1
  89.2 4.3 %fusion = (f32[128,8]{0,1:T(8,128)S(1)}, f32[128,8,2560]{2,0,1:T(8,128)S(1)}) fusion(pred[128,2560]{1,0:T(8,128)(4,1)S(1)} %compare_select_fusion, bf16[2560,256]{1,0:T(8,128)(2,1)} %all-gather.2.cloned.1.call-done, bf16[128,8,128]{2,1,0:T(8,128)(2,1)S(1)} %multiply_convert_fusion), kind=kOutput, calls=%fused_computation.1 | convolution fusion | flops 678951936 | bytes 11735040 | tf_op jit(solution)/shard_map/qhd,kd->qhk/dot_general | solution.py:427
  93.5 0.0 copy-done.1
  93.5 2.0 %fusion.8 = bf16[128,8,128]{0,2,1:T(8,128)(2,1)S(1)} fusion(f32[128,8,2560]{2,0,1:T(8,128)S(1)} %get-tuple-element.6, pred[128,2560]{1,0:T(8,128)(4,1)S(1)} %compare_select_fusion, bf16[2560,256]{1,0:T(8,128)(2,1)S(1)} %copy-done.1, f32[128,8]{0,1:T(8,128)S(1)} %get-tuple-element.5), kind=kOutput, calls=%fused_computation.7 | convolution fusion | flops 679215104 | bytes 11735040 | tf_op jit(solution)/shard_map/qhk,kd->qhd/dot_general | solution.py:431
  95.4 0.8 copy.56.attn_ref
  96.3 86.5 %shard_map.127 = bf16[16,4096]{1,0:T(8,128)(2,1)} custom-call(bf16[128,1024]{1,0:T(8,128)(2,1)} %copy.56.attn_ref, bf16[1024,4096]{1,0:T(8,128)(2,1)} %out_weight_hbm.1, bf16[16,4096]{1,0:T(8,128)(2,1)} %residual_ref.1, f32[1,4096]{1,0:T(1,128)} %bitcast.23, s32[1,512]{1,0:T(1,128)} %reshape_select_fusion.1.place_row_ref, ...), custom_call_target="tpu_custom_call" | custom-call | tf_op jit(solution)/shard_map/pallas_call | solution.py:353
  182.8 1.6 copy.64
  (11 shorter events, 0.1 us)
Async XLA Ops:
  6.5 1.2 copy-start
  6.5 82.6 %all-gather.2.cloned.1.call-start = ((), (), s32[]{:S(2)}) async-start(), calls=%async_computation | async-start | bytes 1638400 | tf_op jit(solution)/shard_map/all_gather | solution.py:415
  89.2 4.3 %copy-start.1 = (bf16[2560,256]{1,0:T(8,128)(2,1)S(1)}, bf16[2560,256]{1,0:T(8,128)(2,1)}, u32[]{:S(2)}) copy-start(bf16[2560,256]{1,0:T(8,128)(2,1)} %all-gather.2.cloned.1.call-done) | copy-start | bytes 3932164
Sparse Core Ops, SparseCore 0:
  10.6 20.8 all-gather.1

commit v2 on v1

--- a/solution.py
+++ b/solution.py
@@ -43,16 +43,29 @@
 
 def layer_kernel(
     dims,
-    attn_ref,
+    queries_hbm,
+    cache_hbm,
+    new_kv_hbm,
+    q_gain_ref,
+    k_gain_ref,
+    limit_ref,
     out_weight_hbm,
     residual_ref,
     gain_ref,
-    place_row_ref,
-    place_col_ref,
-    scale_col_ref,
+    ids_ref,
+    combine_ref,
     gate_up_hbm,
     down_hbm,
     result_ref,
+    queries,
+    keyval,
+    query_normed,
+    mixed,
+    weight_sum,
+    attn,
+    routing,
+    select,
+    spread,
     out_w,
     gate_up,
     down,
@@ -79,15 +92,23 @@
     send_sem,
     recv_sem,
 ):
-    nz, ny, nx, slots = dims
+    nz, ny, nx, capacity = dims
     head, tok = lax.axis_index("head"), lax.axis_index("tok")
     z, y = lax.div(head, ny), lax.rem(head, ny)
     x, core = lax.div(tok, CORES), lax.rem(tok, CORES)
+    tok_count = nx * CORES
     width = hidden.shape[1]
+    rows_out = hidden.shape[0]
     step = width // CHUNKS
-    tokens = place_row_ref.shape[1]
+    slots, tokens = select.shape
+    topk = ids_ref.shape[1]
     hidden_units = down.shape[0]
+    query_rows = queries.shape[0]
+    local_heads = queries.shape[1] // HD
+    cache_rows = cache_hbm.shape[1]
+    segment = keyval.shape[1]
     columns = [pl.ds(k * step, step) for k in range(CHUNKS)]
+    spans = columns[:-1] + [pl.ds(width - step, step + 128)]
 
     axes = {
         "z": (nz, z, lambda p: (p * ny + y, tok)),
@@ -104,6 +125,12 @@
         loads.append(copy)
         return copy
 
+    kv_index = lax.div(head * local_heads, HEADS // KV_HEADS)
+    kv_loads = [
+        load(cache_hbm.at[kv_index], keyval.at[tok, pl.ds(0, cache_rows)]),
+        load(new_kv_hbm.at[kv_index], keyval.at[tok, pl.ds(cache_rows, query_rows)]),
+    ]
+    query_load = load(queries_hbm, queries)
     out_w_loads = [load(out_weight_hbm.at[:, c], out_w.at[:, c]) for c in columns]
     gate_up_loads = [load(gate_up_hbm.at[0, c, :], gate_up.at[c, :]) for c in columns]
     down_loads = [load(down_hbm.at[0, :, c], down.at[:, c]) for c in columns]
@@ -116,7 +143,6 @@
                 barrier, inc=1, device_id=device(lax.rem(me + i, n)), device_id_type=MESH
             )
             greeted += 1
-    pl.semaphore_wait(barrier, greeted)
 
     sends = []
 
@@ -134,6 +160,9 @@
             )
             copy.start()
             sends.append(copy)
+
+    def spread_out(stage, k, axis, place):
+        send(stage, k, axis, lambda _: place, lambda _: place)
 
     def arrive(stage, k, axis, region):
         n, me, device = axes[axis]
@@ -155,100 +184,222 @@
             value = value + other.astype(jnp.float32)
         return value
 
-    for k, c in enumerate(columns):
+    def wavefront(stages):
+        for turn in range(CHUNKS + len(stages) - 1):
+            for place in reversed(range(len(stages))):
+                if 0 <= turn - place < CHUNKS:
+                    stages[place](turn - place)
+
+    routing[tok, z, y, :, :] = jnp.full((rows_out, 256), -1.0, jnp.bfloat16)
+    routing[tok, z, y, :, pl.ds(0, topk)] = (
+        ids_ref[...].astype(jnp.float32).astype(jnp.bfloat16)
+    )
+    routing[tok, z, y, :, pl.ds(128, topk)] = combine_ref[...]
+    for copy in kv_loads:
+        copy.wait()
+    keyval[tok, :, :HD] = rms_scale(
+        keyval[tok, :, :HD].astype(jnp.float32), k_gain_ref[...]
+    ).astype(jnp.bfloat16)
+    pl.semaphore_wait(barrier, greeted)
+    spread_out(0, 0, "x", keyval.at[tok])
+    spread_out(1, 0, "core", keyval.at[tok])
+    spread_out(2, 0, "z", routing.at[tok, z, y])
+    query_load.wait()
+    for j in range(local_heads):
+        query_normed[j] = rms_scale(
+            queries[:, j * HD : (j + 1) * HD].astype(jnp.float32), q_gain_ref[...]
+        ).astype(jnp.bfloat16)
+
+    def attend(owner, first):
+        key_at = lax.broadcasted_iota(jnp.int32, (query_rows, segment), 1)
+        query_at = lax.broadcasted_iota(jnp.int32, (query_rows, segment), 0)
+        seen = jnp.where(
+            key_at < cache_rows,
+            (owner * cache_rows + key_at < limit_ref[...]).astype(jnp.int32),
+            (
+                owner * query_rows + key_at - cache_rows <= tok * query_rows + query_at
+            ).astype(jnp.int32),
+        )
+
+        def one_head(j, _):
+            scores = lax.dot_general(
+                query_normed[j],
+                keyval[owner, :, :HD],
+                (((1,), (1,)), ((), ())),
+                preferred_element_type=jnp.float32,
+            )
+            weights = jnp.where(seen > 0, jnp.exp(scores * HD ** (-0.5)), 0.0)
+            sums = weights[:, :128]
+            for i in range(1, segment // 128):
+                sums = sums + weights[:, i * 128 : (i + 1) * 128]
+            value = dot32(weights.astype(jnp.bfloat16), keyval[owner, :, HD:])
+            weight_sum[j] = sums if first else weight_sum[j] + sums
+            mixed[j] = value if first else mixed[j] + value
+            return 0
+
+        lax.fori_loop(0, local_heads, one_head, 0, unroll=2)
+
+    attend(tok, True)
+    arrive(2, 0, "z", lambda i, p: routing.at[tok, p, y])
+    spread_out(3, 0, "y", routing.at[tok, :, y])
+    arrive(1, 0, "core", lambda i, p: keyval.at[x * CORES + p])
+    attend(x * CORES + 1 - core, False)
+    arrive(3, 0, "y", lambda i, p: routing.at[tok, :, p])
+    spread_out(4, 0, "x", routing.at[tok])
+    arrive(0, 0, "x", lambda i, p: keyval.at[p * CORES + core])
+    for i in range(1, nx):
+        spread_out(1, i, "core", keyval.at[lax.rem(x + nx - i, nx) * CORES + core])
+    for i in range(1, nx):
+        attend(lax.rem(x + nx - i, nx) * CORES + core, False)
+    arrive(4, 0, "x", lambda i, p: routing.at[p * CORES + core])
+    for q in range(nx):
+        spread_out(5, q, "core", routing.at[q * CORES + core])
+    for i in range(1, nx):
+        near = lax.rem(x + nx - i, nx) * CORES
+        arrive(1, i, "core", lambda _, p: keyval.at[near + p])
+        attend(near + 1 - core, False)
+    for j in range(local_heads):
+        attn[:, j * HD : (j + 1) * HD] = (
+            mixed[j] / jnp.sum(weight_sum[j], axis=1, keepdims=True)
+        ).astype(jnp.bfloat16)
+
+    squares = []
+
+    def project(k):
+        c = columns[k]
         out_w_loads[k].wait()
-        proj = dot32(attn_ref[...], out_w[:, c]).astype(jnp.bfloat16)
-        part[:, :, :, c] = proj.reshape(nz, ny, -1, step)
-        send(0, k, "y", lambda p: part.at[:, p, :, c], lambda i: part_y.at[i - 1, :, :, c])
-    for k, c in enumerate(columns):
-        arrive(0, k, "y", lambda i, p: part_y.at[i - 1, :, :, c])
+        proj = dot32(attn[...], out_w[:, c]).astype(jnp.bfloat16)
+        part[:, :, :, c] = proj.reshape(nz, ny, rows_out, step)
+        send(6, k, "y", lambda p: part.at[:, p, :, c], lambda i: part_y.at[i - 1, :, :, c])
+
+    def reduce_y(k):
+        c = columns[k]
+        arrive(6, k, "y", lambda i, p: part_y.at[i - 1, :, :, c])
         value = total(part[:, y, :, c], [part_y[i, :, :, c] for i in range(ny - 1)])
         sum_y[:, :, c] = value.astype(jnp.bfloat16)
-        send(1, k, "z", lambda p: sum_y.at[p, :, c], lambda i: part_z.at[i - 1, :, c])
-    square = jnp.zeros((hidden.shape[0], 1), jnp.float32)
-    for k, c in enumerate(columns):
-        arrive(1, k, "z", lambda i, p: part_z.at[i - 1, :, c])
+        send(7, k, "z", lambda p: sum_y.at[p, :, c], lambda i: part_z.at[i - 1, :, c])
+
+    def reduce_z(k):
+        c = columns[k]
+        arrive(7, k, "z", lambda i, p: part_z.at[i - 1, :, c])
         value = total(sum_y[z, :, c], [part_z[i, :, c] for i in range(nz - 1)])
         value = value + residual_ref[:, c].astype(jnp.float32)
         hidden[:, c] = value
-        square = square + jnp.sum(value * value, axis=1, keepdims=True)
-    scale = lax.rsqrt(square / width + EPSILON)
-
-    for k, c in enumerate(columns):
-        rows[tok, z, y, :, c] = (hidden[:, c] * scale * gain_ref[:, c]).astype(jnp.bfloat16)
-        mine = lambda _: rows.at[tok, z, y, :, c]
-        send(2, k, "z", mine, mine)
-    for k, c in enumerate(columns):
-        arrive(2, k, "z", lambda i, p: rows.at[tok, p, y, :, c])
-        mine = lambda _: rows.at[tok, :, y, :, c]
-        send(3, k, "xy"[k % 2], mine, mine)
-    for k, c in enumerate(columns):
-        if k % 2 == 0:
-            arrive(3, k, "x", lambda i, p: rows.at[p * CORES + core, :, y, :, c])
-            for q in range(nx):
-                mine = lambda _: rows.at[q * CORES + core, :, y, :, c]
-                send(4 + q, k, "y", mine, mine)
-        else:
-            arrive(3, k, "y", lambda i, p: rows.at[tok, :, p, :, c])
-            mine = lambda _: rows.at[tok, :, :, :, c]
-            send(4, k, "x", mine, mine)
-    base = 4 + nx
-    for k, c in enumerate(columns):
-        if k % 2 == 0:
-            for q in range(nx):
-                arrive(4 + q, k, "y", lambda i, p: rows.at[q * CORES + core, :, p, :, c])
-        else:
-            arrive(4, k, "x", lambda i, p: rows.at[p * CORES + core, :, :, :, c])
+        squares.append(jnp.sum(value * value, axis=1, keepdims=True))
+        rows[tok, z, y, :, c] = (value * gain_ref[:, c]).astype(jnp.bfloat16)
+        if k == CHUNKS - 1:
+            scale = lax.rsqrt(sum(squares) / width + EPSILON)
+            high = scale.astype(jnp.bfloat16).astype(jnp.float32)
+            lane = lax.broadcasted_iota(jnp.int32, (rows_out, 128), 1)
+            both = jnp.where(lane == 0, high, jnp.where(lane == 1, scale - high, 0.0))
+            rows[tok, z, y, :, pl.ds(width, 128)] = both.astype(jnp.bfloat16)
+        spread_out(8, k, "z", rows.at[tok, z, y, :, spans[k]])
+
+    def gather_z(k):
+        c = spans[k]
+        arrive(8, k, "z", lambda i, p: rows.at[tok, p, y, :, c])
+        spread_out(9, k, "y", rows.at[tok, :, y, :, c])
+
+    def gather_y(k):
+        c = spans[k]
+        arrive(9, k, "y", lambda i, p: rows.at[tok, :, p, :, c])
+        spread_out(10, k, "x", rows.at[tok, :, :, :, c])
+        spread_out(11, k, "core", rows.at[tok, :, :, :, c])
+
+    def gather_x(k):
+        c = spans[k]
+        arrive(10, k, "x", lambda i, p: rows.at[p * CORES + core, :, :, :, c])
+        for i in range(1, nx):
+            far = lax.rem(x + nx - i, nx) * CORES + core
+            spread_out(11 + i, k, "core", rows.at[far, :, :, :, c])
+
+    def up(k):
+        c = spans[k]
+        arrive(11, k, "core", lambda i, p: rows.at[x * CORES + p, :, :, :, c])
+        for i in range(1, nx):
+            near = lax.rem(x + nx - i, nx) * CORES
+            arrive(11 + i, k, "core", lambda _, p: rows.at[near + p, :, :, :, c])
+        picked = dot32(select[...], rows[:, :, :, :, c].reshape(tokens, -1))
+        gate_up_loads[k].wait()
+        both = dot32(picked[:, :step].astype(jnp.bfloat16), gate_up[columns[k], :])
+        both = both if k == 0 else acc[...] + both
+        if k == CHUNKS - 1:
+            both = both * jnp.sum(picked[:, step:], axis=1, keepdims=True)
+        acc[...] = both
+
+    def place_rows():
         for q in range(nx):
-            mine = lambda _: rows.at[q * CORES + core, :, :, :, c]
-            send(base + q, k, "core", mine, mine)
-    select = (
-        lax.broadcasted_iota(jnp.int32, (slots, tokens), 0) == place_row_ref[...]
-    ).astype(jnp.bfloat16)
-    for k, c in enumerate(columns):
-        for q in range(nx):
-            arrive(base + q, k, "core", lambda i, p: rows.at[q * CORES + p, :, :, :, c])
-        picked = dot32(select, rows[:, :, :, :, c].reshape(tokens, step)).astype(jnp.bfloat16)
-        gate_up_loads[k].wait()
-        both = dot32(picked, gate_up[c, :])
-        acc[...] = both if k == 0 else acc[...] + both
-    base += nx
+            arrive(5, q, "core", lambda i, p: routing.at[q * CORES + p])
+        own = (head * tok_count + tok).astype(jnp.float32)
+        flat = routing[...].reshape(tokens, 256).astype(jnp.float32)
+        named = flat[:, :128] == own
+        chosen = jnp.sum(jnp.where(named, 1.0, 0.0), axis=1, keepdims=True)
+        scale = jnp.sum(jnp.where(named, flat[:, 128:], 0.0), axis=1, keepdims=True)
+        here = lax.broadcasted_iota(jnp.int32, (tokens, tokens), 0)
+        there = lax.broadcasted_iota(jnp.int32, (tokens, tokens), 1)
+        earlier = (there < here) & (there >= here - lax.rem(here, rows_out))
+        before = dot32(
+            jnp.where(earlier, 1.0, 0.0).astype(jnp.bfloat16),
+            jnp.broadcast_to(chosen, (tokens, 128)).astype(jnp.bfloat16),
+        )[:, :1]
+        at = lax.broadcasted_iota(jnp.int32, (tokens, 1), 0)
+        start = lax.div(at, rows_out) * capacity
+        place = jnp.where(chosen > 0.0, start.astype(jnp.float32) + before, -1.0)
+        slot = lax.broadcasted_iota(jnp.int32, (tokens, slots), 1)
+        hit = slot == place.astype(jnp.int32)
+        spread[...] = jnp.where(hit, scale, 0.0).astype(jnp.bfloat16)
+        select[...] = jnp.where(hit, 1.0, 0.0).T.astype(jnp.bfloat16)
+
+    def first_up(k):
+        if k == 0:
+            place_rows()
+        gather_z(k)
+
+    wavefront([project, reduce_y, reduce_z, first_up, gather_y, gather_x, up])
 
     gate = acc[:, :hidden_units]
     active[...] = (jax.nn.silu(gate) * acc[:, hidden_units:]).astype(jnp.bfloat16)
-    spread = jnp.where(
-        lax.broadcasted_iota(jnp.int32, (tokens, slots), 1) == place_col_ref[...],
-        scale_col_ref[...],
-        0.0,
-    ).astype(jnp.bfloat16)
-
-    for k, c in enumerate(columns):
+
+    base = 11 + nx
+
+    def give(k):
+        c = columns[k]
         down_loads[k].wait()
         expert_out = dot32(active[...], down[:, c]).astype(jnp.bfloat16)
-        weighted = dot32(spread, expert_out).astype(jnp.bfloat16)
-        share[:, :, :, :, :, c] = weighted.reshape(nx, CORES, nz, ny, -1, step)
+        weighted = dot32(spread[...], expert_out).astype(jnp.bfloat16)
+        share[:, :, :, :, :, c] = weighted.reshape(nx, CORES, nz, ny, rows_out, step)
         send(
-            base, k, "core",
+            base,
+            k,
+            "core",
             lambda p: share.at[:, p, :, :, :, c],
             lambda i: in_core.at[:, :, :, :, c],
         )
-    for k, c in enumerate(columns):
+
+    def return_core(k):
+        c = columns[k]
         arrive(base, k, "core", lambda i, p: in_core.at[:, :, :, :, c])
         value = total(share[:, core, :, :, :, c], [in_core[:, :, :, :, c]])
         sum_core[:, :, :, :, c] = value.astype(jnp.bfloat16)
         if k % 2 == 0:
             send(
-                base + 1, k, "x",
+                base + 1,
+                k,
+                "x",
                 lambda p: sum_core.at[p, :, :, :, c],
                 lambda i: in_ax.at[i - 1, :, :, :, c],
             )
         else:
             send(
-                base + 1, k, "y",
+                base + 1,
+                k,
+                "y",
                 lambda p: sum_core.at[:, :, p, :, c],
                 lambda i: in_ay.at[i - 1, :, :, :, c],
             )
-    for k, c in enumerate(columns):
+
+    def return_first(k):
+        c = columns[k]
         if k % 2 == 0:
             arrive(base + 1, k, "x", lambda i, p: in_ax.at[i - 1, :, :, :, c])
             value = total(
@@ -256,7 +407,9 @@
             )
             sum_ax[:, :, :, c] = value.astype(jnp.bfloat16)
             send(
-                base + 2, k, "y",
+                base + 2,
+                k,
+                "y",
                 lambda p: sum_ax.at[:, p, :, c],
                 lambda i: in_by.at[i - 1, :, :, c],
             )
@@ -267,11 +420,15 @@
             )
             sum_ay[:, :, :, c] = value.astype(jnp.bfloat16)
             send(
-                base + 2, k, "x",
+                base + 2,
+                k,
+                "x",
                 lambda p: sum_ay.at[p, :, :, c],
                 lambda i: in_bx.at[i - 1, :, :, c],
             )
-    for k, c in enumerate(columns):
+
+    def return_second(k):
+        c = columns[k]
         if k % 2 == 0:
             arrive(base + 2, k, "y", lambda i, p: in_by.at[i - 1, :, :, c])
             value = total(sum_ax[:, y, :, c], [in_by[i, :, :, c] for i in range(ny - 1)])
@@ -280,16 +437,32 @@
             value = total(sum_ay[x, :, :, c], [in_bx[i, :, :, c] for i in range(nx - 1)])
         sum_b[:, :, c] = value.astype(jnp.bfloat16)
         send(base + 3, k, "z", lambda p: sum_b.at[p, :, c], lambda i: in_z.at[i - 1, :, c])
-    for k, c in enumerate(columns):
+
+    def return_z(k):
+        c = columns[k]
         arrive(base + 3, k, "z", lambda i, p: in_z.at[i - 1, :, c])
         value = total(sum_b[z, :, c], [in_z[i, :, c] for i in range(nz - 1)])
         result_ref[:, c] = (hidden[:, c] + value).astype(jnp.bfloat16)
+
+    wavefront([give, return_core, return_first, return_second, return_z])
     for copy in sends:
         copy.wait_send()
 
 
 def routed_layer(
-    attn, out_weight, residual, norm_gain, expert_ids, combine_weight, w_gate_up, w_down
+    queries,
+    cache,
+    new_kv,
+    q_gain,
+    k_gain,
+    out_weight,
+    residual,
+    norm_gain,
+    expert_ids,
+    combine_weight,
+    prefix_len,
+    w_gate_up,
+    w_down,
 ):
     head_count = lax.axis_size("head")
     tok_count = lax.axis_size("tok")
@@ -302,28 +475,24 @@
     slots = experts_all * capacity
     hidden_units = w_down.shape[1]
 
-    routing = lax.all_gather(
-        jnp.concatenate([expert_ids.astype(jnp.bfloat16), combine_weight], axis=1),
-        ("tok", "head"),
-        axis=0,
-        tiled=True,
-    )
-    own = lax.axis_index("head") * tok_count + lax.axis_index("tok")
-    named = routing[:, :topk].astype(jnp.int32) == own
-    chosen = jnp.any(named, axis=1)
-    scale = jnp.sum(jnp.where(named, routing[:, topk:].astype(jnp.float32), 0.0), axis=1)
-    blocks = chosen.reshape(experts_all, rows_out).astype(jnp.int32)
-    earlier = jnp.arange(rows_out)[:, None] < jnp.arange(rows_out)[None, :]
-    before = jnp.sum(jnp.where(earlier[None], blocks[:, :, None], 0), axis=1)
-    place = jnp.arange(experts_all, dtype=jnp.int32)[:, None] * capacity + before
-    place = jnp.where(chosen, place.reshape(-1), -1)
-
     b16, f32 = jnp.bfloat16, jnp.float32
     vmem = pl.BlockSpec(memory_space=pltpu.VMEM)
     hbm = pl.BlockSpec(memory_space=pl.ANY)
-    stages = 8 + 2 * nx
+    stages = 15 + nx
+    query_rows = queries.shape[0]
+    heads = queries.shape[1] // HD
+    segment = cache.shape[1] + query_rows
     widest = max(nz, ny, nx, CORES) - 1
     scratch = [
+        pltpu.VMEM(queries.shape, b16),
+        pltpu.VMEM((tok_count, segment, 2 * HD), b16),
+        pltpu.VMEM((heads, query_rows, HD), b16),
+        pltpu.VMEM((heads, query_rows, HD), f32),
+        pltpu.VMEM((heads, query_rows, 128), f32),
+        pltpu.VMEM(queries.shape, b16),
+        pltpu.VMEM((tok_count, nz, ny, rows_out, 256), b16),
+        pltpu.VMEM((slots, tokens), b16),
+        pltpu.VMEM((tokens, slots), b16),
         pltpu.VMEM(out_weight.shape, b16),
         pltpu.VMEM(w_gate_up.shape[1:], b16),
         pltpu.VMEM(w_down.shape[1:], b16),
@@ -332,7 +501,7 @@
         pltpu.VMEM((nz, rows_out, width), b16),
         pltpu.VMEM((nz - 1, rows_out, width), b16),
         pltpu.VMEM((rows_out, width), f32),
-        pltpu.VMEM((tok_count, nz, ny, rows_out, width), b16),
+        pltpu.VMEM((tok_count, nz, ny, rows_out, width + 128), b16),
         pltpu.VMEM((slots, 2 * hidden_units), f32),
         pltpu.VMEM((slots, hidden_units), b16),
         pltpu.VMEM((nx, CORES, nz, ny, rows_out, width), b16),
@@ -346,27 +515,31 @@
         pltpu.VMEM((ny - 1, nz, rows_out, width), b16),
         pltpu.VMEM((nz, rows_out, width), b16),
         pltpu.VMEM((nz - 1, rows_out, width), b16),
-        pltpu.SemaphoreType.DMA((3 * CHUNKS,)),
+        pltpu.SemaphoreType.DMA((3 + 3 * CHUNKS,)),
         pltpu.SemaphoreType.DMA((stages, CHUNKS, widest)),
         pltpu.SemaphoreType.DMA((stages, CHUNKS, widest)),
     ]
     return pl.pallas_call(
-        functools.partial(layer_kernel, (nz, ny, nx, slots)),
+        functools.partial(layer_kernel, (nz, ny, nx, capacity)),
         out_shape=jax.ShapeDtypeStruct((rows_out, width), b16),
-        in_specs=[vmem, hbm, vmem, vmem, vmem, vmem, vmem, hbm, hbm],
+        in_specs=[hbm] * 3 + [vmem] * 3 + [hbm] + [vmem] * 4 + [hbm] * 2,
         out_specs=vmem,
         scratch_shapes=scratch,
         compiler_params=pltpu.CompilerParams(
             collective_id=0, has_side_effects=True, vmem_limit_bytes=VMEM_BYTES
         ),
     )(
-        attn,
+        queries,
+        cache,
+        new_kv,
+        q_gain.reshape(1, HD),
+        k_gain.reshape(1, HD),
+        prefix_len.reshape(1, 1),
         out_weight,
         residual,
         norm_gain.reshape(1, width),
-        place.reshape(1, tokens),
-        place.reshape(tokens, 1),
-        scale.reshape(tokens, 1),
+        expert_ids,
+        combine_weight,
         w_gate_up,
         w_down,
     )
@@ -394,6 +567,22 @@
     head_count = lax.axis_size("head")
     tok_count = lax.axis_size("tok")
     query_rows = queries.shape[0]
+    if fits(query_rows * tok_count, out_weight.shape[1], head_count * tok_count):
+        return routed_layer(
+            queries,
+            cache,
+            new_kv,
+            q_gain,
+            k_gain,
+            out_weight,
+            residual,
+            norm_gain,
+            expert_ids,
+            combine_weight,
+            prefix_len,
+            w_gate_up,
+            w_down,
+        )
     local_heads = queries.shape[1] // HD
     cache_rows = cache.shape[1]
     segment = cache_rows + query_rows
@@ -437,11 +626,6 @@
     total = jnp.sum(weights, axis=2)
     accum, total = (accum, total)
     attn = (accum / total[:, :, None]).astype(jnp.bfloat16).reshape(query_rows, local_heads * HD)
-    experts_total = head_count * tok_count
-    if fits(query_rows * tok_count, out_weight.shape[1], experts_total):
-        return routed_layer(
-            attn, out_weight, residual, norm_gain, expert_ids, combine_weight, w_gate_up, w_down
-        )
     rows_out = query_rows // head_count
     full_proj = lax.psum(
         jnp.dot(attn, out_weight, preferred_element_type=jnp.float32).astype(jnp.bfloat16), "head"

time: 192 us -> 121 us (0.63)
  blocking collectives: 70.6 us -> 0 us
  Pallas kernels: 86.5 us -> 116 us
  between operations: 14.2 us -> 0.66 us
  other arithmetic: 7.45 us -> 0 us
  matrix products: 6.22 us -> 0 us
  local copies, waits for them, and re-layouts: 6.19 us -> 4.26 us
    all_gather x1 -> x0, blocking collectives: 70.6 us -> none  [routed_layer(): lax.all_gather(jnp.concatenate([expert_ids.astype(jnp.bfloat16), combine_...]
    pallas_call x1, Pallas kernels: 86.5 us -> 116 us  [routed_layer(): pl.pallas_call(functools.partial(layer_kernel, (nz, ny, nx, capacity)), o...]
    dot_general x2 -> x0, matrix products: 6.22 us -> none  [the longest x1 4.25 us: per_device(): jnp.einsum('qhd,kd->qhk', query_normed, piece[:, :HD], preferred_element_...]
    convert_element_type x4 -> x0, other arithmetic: 2.36 us -> none  [the longest x1 0.86 us: per_device(): query_normed = rms_scale(queries.reshape(query_rows, local_heads, HD).ast...]
    unnamed x6 -> x3, local copies, waits for them, and re-layouts: 2.89 us -> 4.26 us
  transfers between devices with their start and end apart: 1 -> 0, of which waited for: 0 -> 0; matrix products, arithmetic and copies ran while one was open for 4% -> 0% of each run, Pallas kernels for 0% -> 0%
where the time goes in v2:
time: 121 us
  Pallas kernels  116 us (96%)
  local copies, waits for them, and re-layouts  4.26 us (4%)
    pallas_call x1, Pallas kernels, routed_layer(): pl.pallas_call(functools.partial(layer_kernel, (nz, ny, nx, capacity)), o...  116 us
    unnamed x3, local copies, waits for them, and re-layouts  4.26 us

profile of v2, /device:TPU:0, one launch (start us, length us, event | category | flops | bytes accessed | tf_op | source)
XLA Modules:
  0.0 121.0 jit_solution(3961275656156088803)
XLA Ops:
  0.7 1.3 %copy.15.combine_ref = bf16[16,8]{1,0:T(8,128)(2,1)} copy(bf16[16,8]{0,1:T(8,128)(2,1)} %param.22) | data formatting | bytes 512 | tf_op args[9]
  2.0 1.4 %copy.14.ids_ref = s32[16,8]{1,0:T(8,128)} copy(s32[16,8]{0,1:T(8,128)} %param.21) | data formatting | bytes 1024 | tf_op args[8]
  3.3 116.1 %shard_map.127 = bf16[16,4096]{1,0:T(8,128)(2,1)} custom-call(bf16[128,1024]{1,0:T(8,128)(2,1)} %queries_hbm.1, bf16[4,512,256]{2,1,0:T(8,128)(2,1)} %cache_hbm.1, bf16[4,128,256]{2,1,0:T(8,128)(2,1)} %new_kv_hbm.1, f32[1,128]{1,0:T(1,128)} %bitcast.6, f32[1,128]{1,0:T(1,128)} %bitcast.7, s32[1,1]{1,0:T(1,128)} %bitcast.4.limit_ref, ...), custom_call_target="tpu_custom_call" | custom-call | tf_op jit(solution)/shard_map/pallas_call | solution.py:522
  119.4 1.6 %copy.18 = bf16[16,4096]{1,0:T(8,128)(2,1)} copy(bf16[16,4096]{1,0:T(8,128)(2,1)} %shard_map.127) | data formatting | bytes 262144

commit v3 on v2

--- a/solution.py
+++ b/solution.py
@@ -32,7 +32,9 @@
 
 DEPTH = 4
 CORES = 2
-CHUNKS = 4
+CHUNKS = 8
+GROUP = 4
+FLIGHT = 2
 VMEM_BYTES = 60 * 2**20
 MESH = pl.DeviceIdType.MESH
 
@@ -101,7 +103,7 @@
     rows_out = hidden.shape[0]
     step = width // CHUNKS
     slots, tokens = select.shape
-    topk = ids_ref.shape[1]
+    topk = ids_ref.shape[0]
     hidden_units = down.shape[0]
     query_rows = queries.shape[0]
     local_heads = queries.shape[1] // HD
@@ -185,16 +187,25 @@
         return value
 
     def wavefront(stages):
-        for turn in range(CHUNKS + len(stages) - 1):
+        for turn in range(CHUNKS + FLIGHT * (len(stages) - 1)):
             for place in reversed(range(len(stages))):
-                if 0 <= turn - place < CHUNKS:
-                    stages[place](turn - place)
-
-    routing[tok, z, y, :, :] = jnp.full((rows_out, 256), -1.0, jnp.bfloat16)
-    routing[tok, z, y, :, pl.ds(0, topk)] = (
-        ids_ref[...].astype(jnp.float32).astype(jnp.bfloat16)
-    )
-    routing[tok, z, y, :, pl.ds(128, topk)] = combine_ref[...]
+                if 0 <= turn - FLIGHT * place < CHUNKS:
+                    stages[place](turn - FLIGHT * place)
+
+    lane = lax.broadcasted_iota(jnp.int32, (topk, 128), 1)
+    turned = jnp.where(lane == lax.broadcasted_iota(jnp.int32, (topk, 128), 0), 1.0, 0.0)
+    empty = lax.broadcasted_iota(jnp.int32, (rows_out, 128), 1) >= topk
+
+    def by_row(ref):
+        return lax.dot_general(
+            ref[...].astype(jnp.float32),
+            turned,
+            (((0,), (0,)), ((), ())),
+            preferred_element_type=jnp.float32,
+        )
+
+    routing[tok, z, y, :, :128] = jnp.where(empty, -1.0, by_row(ids_ref)).astype(jnp.bfloat16)
+    routing[tok, z, y, :, 128:] = by_row(combine_ref).astype(jnp.bfloat16)
     for copy in kv_loads:
         copy.wait()
     keyval[tok, :, :HD] = rms_scale(
@@ -206,7 +217,7 @@
     spread_out(2, 0, "z", routing.at[tok, z, y])
     query_load.wait()
     for j in range(local_heads):
-        query_normed[j] = rms_scale(
+        query_normed[j * query_rows : (j + 1) * query_rows] = rms_scale(
             queries[:, j * HD : (j + 1) * HD].astype(jnp.float32), q_gain_ref[...]
         ).astype(jnp.bfloat16)
 
@@ -221,23 +232,23 @@
             ).astype(jnp.int32),
         )
 
-        def one_head(j, _):
+        for j in range(0, local_heads * query_rows, GROUP * query_rows):
+            part_rows = pl.ds(j, GROUP * query_rows)
             scores = lax.dot_general(
-                query_normed[j],
+                query_normed[part_rows],
                 keyval[owner, :, :HD],
                 (((1,), (1,)), ((), ())),
                 preferred_element_type=jnp.float32,
             )
-            weights = jnp.where(seen > 0, jnp.exp(scores * HD ** (-0.5)), 0.0)
+            scores = (scores * HD ** (-0.5)).reshape(GROUP, query_rows, segment)
+            weights = jnp.where(seen[None] > 0, jnp.exp(scores), 0.0)
+            weights = weights.reshape(GROUP * query_rows, segment)
             sums = weights[:, :128]
             for i in range(1, segment // 128):
                 sums = sums + weights[:, i * 128 : (i + 1) * 128]
             value = dot32(weights.astype(jnp.bfloat16), keyval[owner, :, HD:])
-            weight_sum[j] = sums if first else weight_sum[j] + sums
-            mixed[j] = value if first else mixed[j] + value
-            return 0
-
-        lax.fori_loop(0, local_heads, one_head, 0, unroll=2)
+            weight_sum[part_rows] = sums if first else weight_sum[part_rows] + sums
+            mixed[part_rows] = value if first else mixed[part_rows] + value
 
     attend(tok, True)
     arrive(2, 0, "z", lambda i, p: routing.at[tok, p, y])
@@ -259,8 +270,9 @@
         arrive(1, i, "core", lambda _, p: keyval.at[near + p])
         attend(near + 1 - core, False)
     for j in range(local_heads):
+        mine = pl.ds(j * query_rows, query_rows)
         attn[:, j * HD : (j + 1) * HD] = (
-            mixed[j] / jnp.sum(weight_sum[j], axis=1, keepdims=True)
+            mixed[mine] / jnp.sum(weight_sum[mine], axis=1, keepdims=True)
         ).astype(jnp.bfloat16)
 
     squares = []
@@ -271,6 +283,8 @@
         proj = dot32(attn[...], out_w[:, c]).astype(jnp.bfloat16)
         part[:, :, :, c] = proj.reshape(nz, ny, rows_out, step)
         send(6, k, "y", lambda p: part.at[:, p, :, c], lambda i: part_y.at[i - 1, :, :, c])
+        if k == FLIGHT - 1:
+            place_rows()
 
     def reduce_y(k):
         c = columns[k]
@@ -350,12 +364,7 @@
         spread[...] = jnp.where(hit, scale, 0.0).astype(jnp.bfloat16)
         select[...] = jnp.where(hit, 1.0, 0.0).T.astype(jnp.bfloat16)
 
-    def first_up(k):
-        if k == 0:
-            place_rows()
-        gather_z(k)
-
-    wavefront([project, reduce_y, reduce_z, first_up, gather_y, gather_x, up])
+    wavefront([project, reduce_y, reduce_z, gather_z, gather_y, gather_x, up])
 
     gate = acc[:, :hidden_units]
     active[...] = (jax.nn.silu(gate) * acc[:, hidden_units:]).astype(jnp.bfloat16)
@@ -486,9 +495,9 @@
     scratch = [
         pltpu.VMEM(queries.shape, b16),
         pltpu.VMEM((tok_count, segment, 2 * HD), b16),
-        pltpu.VMEM((heads, query_rows, HD), b16),
-        pltpu.VMEM((heads, query_rows, HD), f32),
-        pltpu.VMEM((heads, query_rows, 128), f32),
+        pltpu.VMEM((heads * query_rows, HD), b16),
+        pltpu.VMEM((heads * query_rows, HD), f32),
+        pltpu.VMEM((heads * query_rows, 128), f32),
         pltpu.VMEM(queries.shape, b16),
         pltpu.VMEM((tok_count, nz, ny, rows_out, 256), b16),
         pltpu.VMEM((slots, tokens), b16),
@@ -538,14 +547,16 @@
         out_weight,
         residual,
         norm_gain.reshape(1, width),
-        expert_ids,
-        combine_weight,
+        expert_ids.T,
+        combine_weight.T,
         w_gate_up,
         w_down,
     )
 
 
-def fits(tokens, width, experts):
+def fits(tokens, width, experts, spans, heads):
+    if spans > CORES * CHUNKS or heads % GROUP:
+        return False
     return 12 * tokens * width <= VMEM_BYTES // 2 and experts <= 256
 
 
@@ -567,7 +578,10 @@
     head_count = lax.axis_size("head")
     tok_count = lax.axis_size("tok")
     query_rows = queries.shape[0]
-    if fits(query_rows * tok_count, out_weight.shape[1], head_count * tok_count):
+    local_heads = queries.shape[1] // HD
+    experts_all = head_count * tok_count
+    tokens = query_rows * tok_count
+    if fits(tokens, out_weight.shape[1], experts_all, tok_count, local_heads):
         return routed_layer(
             queries,
             cache,
@@ -583,7 +597,6 @@
             w_gate_up,
             w_down,
         )
-    local_heads = queries.shape[1] // HD
     cache_rows = cache.shape[1]
     segment = cache_rows + query_rows
     kv_index = lax.axis_index("head") * local_heads // (HEADS // KV_HEADS)

time: 121 us -> 101 us (0.83)
  Pallas kernels: 116 us -> 98.9 us
  local copies, waits for them, and re-layouts: 4.26 us -> 1.57 us
    pallas_call x1, Pallas kernels: 116 us -> 98.9 us  [routed_layer(): pl.pallas_call(functools.partial(layer_kernel, (nz, ny, nx, capacity)), o...]
    unnamed x3 -> x1, local copies, waits for them, and re-layouts: 4.26 us -> 1.57 us
where the time goes in v3:
time: 101 us
  Pallas kernels  98.9 us (98%)
  local copies, waits for them, and re-layouts  1.57 us (2%)
    pallas_call x1, Pallas kernels, routed_layer(): pl.pallas_call(functools.partial(layer_kernel, (nz, ny, nx, capacity)), o...  98.9 us

profile of v3, /device:TPU:0, one launch (start us, length us, event | category | flops | bytes accessed | tf_op | source)
XLA Modules:
  0.0 101.2 jit_solution(14093343266574500368)
XLA Ops:
  0.7 98.9 %shard_map.127 = bf16[16,4096]{1,0:T(8,128)(2,1)} custom-call(bf16[128,1024]{1,0:T(8,128)(2,1)} %queries_hbm.1, bf16[4,512,256]{2,1,0:T(8,128)(2,1)} %cache_hbm.1, bf16[4,128,256]{2,1,0:T(8,128)(2,1)} %new_kv_hbm.1, f32[1,128]{1,0:T(1,128)} %bitcast.10, f32[1,128]{1,0:T(1,128)} %bitcast.11, s32[1,1]{1,0:T(1,128)} %bitcast.6.limit_ref, ...), custom_call_target="tpu_custom_call" | custom-call | tf_op jit(solution)/shard_map/pallas_call | solution.py:531
  99.6 1.6 %copy.16 = bf16[16,4096]{1,0:T(8,128)(2,1)} copy(bf16[16,4096]{1,0:T(8,128)(2,1)} %shard_map.127) | data formatting | bytes 262144

commit v4 on v3

--- a/solution.py
+++ b/solution.py
@@ -95,6 +95,7 @@
     recv_sem,
 ):
     nz, ny, nx, capacity = dims
+    extra = 15 + nx
     head, tok = lax.axis_index("head"), lax.axis_index("tok")
     z, y = lax.div(head, ny), lax.rem(head, ny)
     x, core = lax.div(tok, CORES), lax.rem(tok, CORES)
@@ -187,10 +188,10 @@
         return value
 
     def wavefront(stages):
-        for turn in range(CHUNKS + FLIGHT * (len(stages) - 1)):
-            for place in reversed(range(len(stages))):
-                if 0 <= turn - FLIGHT * place < CHUNKS:
-                    stages[place](turn - FLIGHT * place)
+        for turn in range(CHUNKS + stages[-1][0]):
+            for offset, stage in reversed(stages):
+                if 0 <= turn - offset < CHUNKS:
+                    stage(turn - offset)
 
     lane = lax.broadcasted_iota(jnp.int32, (topk, 128), 1)
     turned = jnp.where(lane == lax.broadcasted_iota(jnp.int32, (topk, 128), 0), 1.0, 0.0)
@@ -309,23 +310,38 @@
             rows[tok, z, y, :, pl.ds(width, 128)] = both.astype(jnp.bfloat16)
         spread_out(8, k, "z", rows.at[tok, z, y, :, spans[k]])
 
+    def far(i):
+        return lax.rem(x + nx - i, nx) * CORES + core
+
     def gather_z(k):
         c = spans[k]
         arrive(8, k, "z", lambda i, p: rows.at[tok, p, y, :, c])
-        spread_out(9, k, "y", rows.at[tok, :, y, :, c])
-
-    def gather_y(k):
+        spread_out(9, k, "yx"[k % 2], rows.at[tok, :, y, :, c])
+        if k % 2:
+            spread_out(10, k, "y", rows.at[tok, :, y, :, c])
+
+    def gather_first(k):
         c = spans[k]
-        arrive(9, k, "y", lambda i, p: rows.at[tok, :, p, :, c])
-        spread_out(10, k, "x", rows.at[tok, :, :, :, c])
-        spread_out(11, k, "core", rows.at[tok, :, :, :, c])
-
-    def gather_x(k):
+        if k % 2 == 0:
+            arrive(9, k, "y", lambda i, p: rows.at[tok, :, p, :, c])
+            spread_out(10, k, "x", rows.at[tok, :, :, :, c])
+            spread_out(11, k, "core", rows.at[tok, :, :, :, c])
+        else:
+            arrive(9, k, "x", lambda i, p: rows.at[p * CORES + core, :, y, :, c])
+            for i in range(1, nx):
+                spread_out(extra + i, k, "y", rows.at[far(i), :, y, :, c])
+
+    def gather_second(k):
         c = spans[k]
-        arrive(10, k, "x", lambda i, p: rows.at[p * CORES + core, :, :, :, c])
+        if k % 2 == 0:
+            arrive(10, k, "x", lambda i, p: rows.at[p * CORES + core, :, :, :, c])
+        else:
+            arrive(10, k, "y", lambda i, p: rows.at[tok, :, p, :, c])
+            spread_out(11, k, "core", rows.at[tok, :, :, :, c])
+            for i in range(1, nx):
+                arrive(extra + i, k, "y", lambda _, p: rows.at[far(i), :, p, :, c])
         for i in range(1, nx):
-            far = lax.rem(x + nx - i, nx) * CORES + core
-            spread_out(11 + i, k, "core", rows.at[far, :, :, :, c])
+            spread_out(11 + i, k, "core", rows.at[far(i), :, :, :, c])
 
     def up(k):
         c = spans[k]
@@ -364,7 +380,17 @@
         spread[...] = jnp.where(hit, scale, 0.0).astype(jnp.bfloat16)
         select[...] = jnp.where(hit, 1.0, 0.0).T.astype(jnp.bfloat16)
 
-    wavefront([project, reduce_y, reduce_z, gather_z, gather_y, gather_x, up])
+    wavefront(
+        [
+            (0, project),
+            (FLIGHT, reduce_y),
+            (2 * FLIGHT, reduce_z),
+            (3 * FLIGHT, gather_z),
+            (4 * FLIGHT + 1, gather_first),
+            (5 * FLIGHT + 2, gather_second),
+            (6 * FLIGHT + 2, up),
+        ]
+    )
 
     gate = acc[:, :hidden_units]
     active[...] = (jax.nn.silu(gate) * acc[:, hidden_units:]).astype(jnp.bfloat16)
@@ -453,7 +479,15 @@
         value = total(sum_b[z, :, c], [in_z[i, :, c] for i in range(nz - 1)])
         result_ref[:, c] = (hidden[:, c] + value).astype(jnp.bfloat16)
 
-    wavefront([give, return_core, return_first, return_second, return_z])
+    wavefront(
+        [
+            (0, give),
+            (FLIGHT, return_core),
+            (2 * FLIGHT + 1, return_first),
+            (3 * FLIGHT + 2, return_second),
+            (4 * FLIGHT + 2, return_z),
+        ]
+    )
     for copy in sends:
         copy.wait_send()
 
@@ -487,7 +521,7 @@
     b16, f32 = jnp.bfloat16, jnp.float32
     vmem = pl.BlockSpec(memory_space=pltpu.VMEM)
     hbm = pl.BlockSpec(memory_space=pl.ANY)
-    stages = 15 + nx
+    stages = 15 + 2 * nx
     query_rows = queries.shape[0]
     heads = queries.shape[1] // HD
     segment = cache.shape[1] + query_rows

time: 101 us -> 102 us (level)
  no operation moved by 1% of the time
where the time goes in v4:
time: 102 us; the launch traced here: 101 us
  Pallas kernels  99.1 us (97%)
  local copies, waits for them, and re-layouts  1.57 us (2%)
    pallas_call x1, Pallas kernels, routed_layer(): pl.pallas_call(functools.partial(layer_kernel, (nz, ny, nx, capacity)), o...  99.1 us

profile of v4, /device:TPU:0, one launch (start us, length us, event | category | flops | bytes accessed | tf_op | source)
XLA Modules:
  0.0 101.4 jit_solution(10356455015072702898)
XLA Ops:
  0.7 99.1 %shard_map.127 = bf16[16,4096]{1,0:T(8,128)(2,1)} custom-call(bf16[128,1024]{1,0:T(8,128)(2,1)} %queries_hbm.1, bf16[4,512,256]{2,1,0:T(8,128)(2,1)} %cache_hbm.1, bf16[4,128,256]{2,1,0:T(8,128)(2,1)} %new_kv_hbm.1, f32[1,128]{1,0:T(1,128)} %bitcast.10, f32[1,128]{1,0:T(1,128)} %bitcast.11, s32[1,1]{1,0:T(1,128)} %bitcast.6.limit_ref, ...), custom_call_target="tpu_custom_call" | custom-call | tf_op jit(solution)/shard_map/pallas_call | solution.py:565
  99.8 1.6 %copy.16 = bf16[16,4096]{1,0:T(8,128)(2,1)} copy(bf16[16,4096]{1,0:T(8,128)(2,1)} %shard_map.127) | data formatting | bytes 262144

commit v5 on v4

--- a/solution.py
+++ b/solution.py
@@ -74,6 +74,8 @@
     part,
     part_y,
     sum_y,
+    part_v,
+    sum_v,
     part_z,
     hidden,
     rows,
@@ -89,6 +91,8 @@
     in_bx,
     in_by,
     sum_b,
+    in_v,
+    sum_w,
     in_z,
     load_sem,
     send_sem,
@@ -96,8 +100,10 @@
 ):
     nz, ny, nx, capacity = dims
     extra = 15 + nx
+    more = 15 + 2 * nx
     head, tok = lax.axis_index("head"), lax.axis_index("tok")
     z, y = lax.div(head, ny), lax.rem(head, ny)
+    zh, zl = lax.div(z, 2), lax.rem(z, 2)
     x, core = lax.div(tok, CORES), lax.rem(tok, CORES)
     tok_count = nx * CORES
     width = hidden.shape[1]
@@ -114,7 +120,8 @@
     spans = columns[:-1] + [pl.ds(width - step, step + 128)]
 
     axes = {
-        "z": (nz, z, lambda p: (p * ny + y, tok)),
+        "far_z": (nz // 2, zh, lambda p: ((p * 2 + zl) * ny + y, tok)),
+        "near_z": (2, zl, lambda p: ((zh * 2 + p) * ny + y, tok)),
         "y": (ny, y, lambda p: (z * ny + p, tok)),
         "x": (nx, x, lambda p: (head, p * CORES + core)),
         "core": (CORES, core, lambda p: (head, x * CORES + p)),
@@ -205,8 +212,8 @@
             preferred_element_type=jnp.float32,
         )
 
-    routing[tok, z, y, :, :128] = jnp.where(empty, -1.0, by_row(ids_ref)).astype(jnp.bfloat16)
-    routing[tok, z, y, :, 128:] = by_row(combine_ref).astype(jnp.bfloat16)
+    routing[tok, zh, zl, y, :, :128] = jnp.where(empty, -1.0, by_row(ids_ref)).astype(jnp.bfloat16)
+    routing[tok, zh, zl, y, :, 128:] = by_row(combine_ref).astype(jnp.bfloat16)
     for copy in kv_loads:
         copy.wait()
     keyval[tok, :, :HD] = rms_scale(
@@ -215,7 +222,7 @@
     pl.semaphore_wait(barrier, greeted)
     spread_out(0, 0, "x", keyval.at[tok])
     spread_out(1, 0, "core", keyval.at[tok])
-    spread_out(2, 0, "z", routing.at[tok, z, y])
+    spread_out(2, 0, "far_z", routing.at[tok, zh, zl, y])
     query_load.wait()
     for j in range(local_heads):
         query_normed[j * query_rows : (j + 1) * query_rows] = rms_scale(
@@ -252,11 +259,13 @@
             mixed[part_rows] = value if first else mixed[part_rows] + value
 
     attend(tok, True)
-    arrive(2, 0, "z", lambda i, p: routing.at[tok, p, y])
-    spread_out(3, 0, "y", routing.at[tok, :, y])
+    arrive(2, 0, "far_z", lambda i, p: routing.at[tok, p, zl, y])
+    spread_out(more, 0, "near_z", routing.at[tok, :, zl, y])
     arrive(1, 0, "core", lambda i, p: keyval.at[x * CORES + p])
+    arrive(more, 0, "near_z", lambda i, p: routing.at[tok, :, p, y])
+    spread_out(3, 0, "y", routing.at[tok, :, :, y])
     attend(x * CORES + 1 - core, False)
-    arrive(3, 0, "y", lambda i, p: routing.at[tok, :, p])
+    arrive(3, 0, "y", lambda i, p: routing.at[tok, :, :, p])
     spread_out(4, 0, "x", routing.at[tok])
     arrive(0, 0, "x", lambda i, p: keyval.at[p * CORES + core])
     for i in range(1, nx):
@@ -291,65 +300,81 @@
         c = columns[k]
         arrive(6, k, "y", lambda i, p: part_y.at[i - 1, :, :, c])
         value = total(part[:, y, :, c], [part_y[i, :, :, c] for i in range(ny - 1)])
-        sum_y[:, :, c] = value.astype(jnp.bfloat16)
-        send(7, k, "z", lambda p: sum_y.at[p, :, c], lambda i: part_z.at[i - 1, :, c])
+        sum_y[:, :, :, c] = value.reshape(nz // 2, 2, rows_out, step).astype(jnp.bfloat16)
+        send(
+            7, k, "near_z", lambda p: sum_y.at[:, p, :, c], lambda i: part_v.at[i - 1, :, :, c]
+        )
+
+    def reduce_near(k):
+        c = columns[k]
+        arrive(7, k, "near_z", lambda i, p: part_v.at[i - 1, :, :, c])
+        value = total(sum_y[:, zl, :, c], [part_v[0, :, :, c]])
+        sum_v[:, :, c] = value.astype(jnp.bfloat16)
+        send(
+            more + 1, k, "far_z", lambda p: sum_v.at[p, :, c], lambda i: part_z.at[i - 1, :, c]
+        )
 
     def reduce_z(k):
         c = columns[k]
-        arrive(7, k, "z", lambda i, p: part_z.at[i - 1, :, c])
-        value = total(sum_y[z, :, c], [part_z[i, :, c] for i in range(nz - 1)])
+        arrive(more + 1, k, "far_z", lambda i, p: part_z.at[i - 1, :, c])
+        value = total(sum_v[zh, :, c], [part_z[i, :, c] for i in range(nz // 2 - 1)])
         value = value + residual_ref[:, c].astype(jnp.float32)
         hidden[:, c] = value
         squares.append(jnp.sum(value * value, axis=1, keepdims=True))
-        rows[tok, z, y, :, c] = (value * gain_ref[:, c]).astype(jnp.bfloat16)
+        rows[tok, zh, zl, y, :, c] = (value * gain_ref[:, c]).astype(jnp.bfloat16)
         if k == CHUNKS - 1:
             scale = lax.rsqrt(sum(squares) / width + EPSILON)
             high = scale.astype(jnp.bfloat16).astype(jnp.float32)
             lane = lax.broadcasted_iota(jnp.int32, (rows_out, 128), 1)
             both = jnp.where(lane == 0, high, jnp.where(lane == 1, scale - high, 0.0))
-            rows[tok, z, y, :, pl.ds(width, 128)] = both.astype(jnp.bfloat16)
-        spread_out(8, k, "z", rows.at[tok, z, y, :, spans[k]])
+            rows[tok, zh, zl, y, :, pl.ds(width, 128)] = both.astype(jnp.bfloat16)
+        spread_out(8, k, "far_z", rows.at[tok, zh, zl, y, :, spans[k]])
 
     def far(i):
         return lax.rem(x + nx - i, nx) * CORES + core
 
+    def gather_far(k):
+        c = spans[k]
+        arrive(8, k, "far_z", lambda i, p: rows.at[tok, p, zl, y, :, c])
+        spread_out(more + 2, k, "near_z", rows.at[tok, :, zl, y, :, c])
+
     def gather_z(k):
         c = spans[k]
-        arrive(8, k, "z", lambda i, p: rows.at[tok, p, y, :, c])
-        spread_out(9, k, "yx"[k % 2], rows.at[tok, :, y, :, c])
+        arrive(more + 2, k, "near_z", lambda i, p: rows.at[tok, :, p, y, :, c])
+        spread_out(9, k, "yx"[k % 2], rows.at[tok, :, :, y, :, c])
         if k % 2:
-            spread_out(10, k, "y", rows.at[tok, :, y, :, c])
+            spread_out(10, k, "y", rows.at[tok, :, :, y, :, c])
 
     def gather_first(k):
         c = spans[k]
         if k % 2 == 0:
-            arrive(9, k, "y", lambda i, p: rows.at[tok, :, p, :, c])
-            spread_out(10, k, "x", rows.at[tok, :, :, :, c])
-            spread_out(11, k, "core", rows.at[tok, :, :, :, c])
+            arrive(9, k, "y", lambda i, p: rows.at[tok, :, :, p, :, c])
+            spread_out(10, k, "x", rows.at[tok, :, :, :, :, c])
+            spread_out(11, k, "core", rows.at[tok, :, :, :, :, c])
         else:
-            arrive(9, k, "x", lambda i, p: rows.at[p * CORES + core, :, y, :, c])
+            arrive(9, k, "x", lambda i, p: rows.at[p * CORES + core, :, :, y, :, c])
             for i in range(1, nx):
-                spread_out(extra + i, k, "y", rows.at[far(i), :, y, :, c])
+                spread_out(extra + i, k, "y", rows.at[far(i), :, :, y, :, c])
 
     def gather_second(k):
         c = spans[k]
         if k % 2 == 0:
-            arrive(10, k, "x", lambda i, p: rows.at[p * CORES + core, :, :, :, c])
+            arrive(10, k, "x", lambda i, p: rows.at[p * CORES + core, :, :, :, :, c])
         else:
-            arrive(10, k, "y", lambda i, p: rows.at[tok, :, p, :, c])
-            spread_out(11, k, "core", rows.at[tok, :, :, :, c])
+            arrive(10, k, "y", lambda i, p: rows.at[tok, :, :, p, :, c])
+            spread_out(11, k, "core", rows.at[tok, :, :, :, :, c])
             for i in range(1, nx):
-                arrive(extra + i, k, "y", lambda _, p: rows.at[far(i), :, p, :, c])
+                arrive(extra + i, k, "y", lambda _, p: rows.at[far(i), :, :, p, :, c])
         for i in range(1, nx):
-            spread_out(11 + i, k, "core", rows.at[far(i), :, :, :, c])
+            spread_out(11 + i, k, "core", rows.at[far(i), :, :, :, :, c])
 
     def up(k):
         c = spans[k]
-        arrive(11, k, "core", lambda i, p: rows.at[x * CORES + p, :, :, :, c])
+        arrive(11, k, "core", lambda i, p: rows.at[x * CORES + p, :, :, :, :, c])
         for i in range(1, nx):
             near = lax.rem(x + nx - i, nx) * CORES
-            arrive(11 + i, k, "core", lambda _, p: rows.at[near + p, :, :, :, c])
-        picked = dot32(select[...], rows[:, :, :, :, c].reshape(tokens, -1))
+            arrive(11 + i, k, "core", lambda _, p: rows.at[near + p, :, :, :, :, c])
+        picked = dot32(select[...], rows[:, :, :, :, :, c].reshape(tokens, -1))
         gate_up_loads[k].wait()
         both = dot32(picked[:, :step].astype(jnp.bfloat16), gate_up[columns[k], :])
         both = both if k == 0 else acc[...] + both
@@ -384,11 +409,13 @@
         [
             (0, project),
             (FLIGHT, reduce_y),
-            (2 * FLIGHT, reduce_z),
-            (3 * FLIGHT, gather_z),
-            (4 * FLIGHT + 1, gather_first),
-            (5 * FLIGHT + 2, gather_second),
-            (6 * FLIGHT + 2, up),
+            (2 * FLIGHT, reduce_near),
+            (3 * FLIGHT, reduce_z),
+            (4 * FLIGHT, gather_far),
+            (5 * FLIGHT, gather_z),
+            (6 * FLIGHT + 1, gather_first),
+            (7 * FLIGHT + 2, gather_second),
+            (8 * FLIGHT + 2, up),
         ]
     )
 
@@ -470,13 +497,26 @@
         else:
             arrive(base + 2, k, "x", lambda i, p: in_bx.at[i - 1, :, :, c])
             value = total(sum_ay[x, :, :, c], [in_bx[i, :, :, c] for i in range(nx - 1)])
-        sum_b[:, :, c] = value.astype(jnp.bfloat16)
-        send(base + 3, k, "z", lambda p: sum_b.at[p, :, c], lambda i: in_z.at[i - 1, :, c])
+        sum_b[:, :, :, c] = value.reshape(nz // 2, 2, rows_out, step).astype(jnp.bfloat16)
+        send(
+            base + 3,
+            k,
+            "near_z",
+            lambda p: sum_b.at[:, p, :, c],
+            lambda i: in_v.at[i - 1, :, :, c],
+        )
+
+    def return_near(k):
+        c = columns[k]
+        arrive(base + 3, k, "near_z", lambda i, p: in_v.at[i - 1, :, :, c])
+        value = total(sum_b[:, zl, :, c], [in_v[0, :, :, c]])
+        sum_w[:, :, c] = value.astype(jnp.bfloat16)
+        send(more + 3, k, "far_z", lambda p: sum_w.at[p, :, c], lambda i: in_z.at[i - 1, :, c])
 
     def return_z(k):
         c = columns[k]
-        arrive(base + 3, k, "z", lambda i, p: in_z.at[i - 1, :, c])
-        value = total(sum_b[z, :, c], [in_z[i, :, c] for i in range(nz - 1)])
+        arrive(more + 3, k, "far_z", lambda i, p: in_z.at[i - 1, :, c])
+        value = total(sum_w[zh, :, c], [in_z[i, :, c] for i in range(nz // 2 - 1)])
         result_ref[:, c] = (hidden[:, c] + value).astype(jnp.bfloat16)
 
     wavefront(
@@ -485,7 +525,8 @@
             (FLIGHT, return_core),
             (2 * FLIGHT + 1, return_first),
             (3 * FLIGHT + 2, return_second),
-            (4 * FLIGHT + 2, return_z),
+            (4 * FLIGHT + 2, return_near),
+            (5 * FLIGHT + 2, return_z),
         ]
     )
     for copy in sends:
@@ -521,7 +562,7 @@
     b16, f32 = jnp.bfloat16, jnp.float32
     vmem = pl.BlockSpec(memory_space=pltpu.VMEM)
     hbm = pl.BlockSpec(memory_space=pl.ANY)
-    stages = 15 + 2 * nx
+    stages = 19 + 2 * nx
     query_rows = queries.shape[0]
     heads = queries.shape[1] // HD
     segment = cache.shape[1] + query_rows
@@ -533,7 +574,7 @@
         pltpu.VMEM((heads * query_rows, HD), f32),
         pltpu.VMEM((heads * query_rows, 128), f32),
         pltpu.VMEM(queries.shape, b16),
-        pltpu.VMEM((tok_count, nz, ny, rows_out, 256), b16),
+        pltpu.VMEM((tok_count, nz // 2, 2, ny, rows_out, 256), b16),
         pltpu.VMEM((slots, tokens), b16),
         pltpu.VMEM((tokens, slots), b16),
         pltpu.VMEM(out_weight.shape, b16),
@@ -541,10 +582,12 @@
         pltpu.VMEM(w_down.shape[1:], b16),
         pltpu.VMEM((nz, ny, rows_out, width), b16),
         pltpu.VMEM((ny - 1, nz, rows_out, width), b16),
-        pltpu.VMEM((nz, rows_out, width), b16),
-        pltpu.VMEM((nz - 1, rows_out, width), b16),
+        pltpu.VMEM((nz // 2, 2, rows_out, width), b16),
+        pltpu.VMEM((1, nz // 2, rows_out, width), b16),
+        pltpu.VMEM((nz // 2, rows_out, width), b16),
+        pltpu.VMEM((nz // 2 - 1, rows_out, width), b16),
         pltpu.VMEM((rows_out, width), f32),
-        pltpu.VMEM((tok_count, nz, ny, rows_out, width + 128), b16),
+        pltpu.VMEM((tok_count, nz // 2, 2, ny, rows_out, width + 128), b16),
         pltpu.VMEM((slots, 2 * hidden_units), f32),
         pltpu.VMEM((slots, hidden_units), b16),
         pltpu.VMEM((nx, CORES, nz, ny, rows_out, width), b16),
@@ -556,8 +599,10 @@
         pltpu.VMEM((nx, nz, rows_out, width), b16),
         pltpu.VMEM((nx - 1, nz, rows_out, width), b16),
         pltpu.VMEM((ny - 1, nz, rows_out, width), b16),
-        pltpu.VMEM((nz, rows_out, width), b16),
-        pltpu.VMEM((nz - 1, rows_out, width), b16),
+        pltpu.VMEM((nz // 2, 2, rows_out, width), b16),
+        pltpu.VMEM((1, nz // 2, rows_out, width), b16),
+        pltpu.VMEM((nz // 2, rows_out, width), b16),
+        pltpu.VMEM((nz // 2 - 1, rows_out, width), b16),
         pltpu.SemaphoreType.DMA((3 + 3 * CHUNKS,)),
         pltpu.SemaphoreType.DMA((stages, CHUNKS, widest)),
         pltpu.SemaphoreType.DMA((stages, CHUNKS, widest)),

time: 102 us -> 106 us (1.039)
  Pallas kernels: 99.1 us -> 103 us
    pallas_call x1, Pallas kernels: 99.1 us -> 103 us  [routed_layer(): pl.pallas_call(functools.partial(layer_kernel, (nz, ny, nx, capacity)), o...]
where the time goes in v5:
time: 106 us; the launch traced here: 105 us
  Pallas kernels  103 us (97%)
  local copies, waits for them, and re-layouts  1.57 us (1%)
    pallas_call x1, Pallas kernels, routed_layer(): pl.pallas_call(functools.partial(layer_kernel, (nz, ny, nx, capacity)), o...  103 us

profile of v5, /device:TPU:0, one launch (start us, length us, event | category | flops | bytes accessed | tf_op | source)
XLA Modules:
  0.0 105.4 jit_solution(5733856634647116408)
XLA Ops:
  0.7 103.1 %shard_map.127 = bf16[16,4096]{1,0:T(8,128)(2,1)} custom-call(bf16[128,1024]{1,0:T(8,128)(2,1)} %queries_hbm.1, bf16[4,512,256]{2,1,0:T(8,128)(2,1)} %cache_hbm.1, bf16[4,128,256]{2,1,0:T(8,128)(2,1)} %new_kv_hbm.1, f32[1,128]{1,0:T(1,128)} %bitcast.10, f32[1,128]{1,0:T(1,128)} %bitcast.11, s32[1,1]{1,0:T(1,128)} %bitcast.6.limit_ref, ...), custom_call_target="tpu_custom_call" | custom-call | tf_op jit(solution)/shard_map/pallas_call | solution.py:610
  103.8 1.6 %copy.16 = bf16[16,4096]{1,0:T(8,128)(2,1)} copy(bf16[16,4096]{1,0:T(8,128)(2,1)} %shard_map.127) | data formatting | bytes 262144
